TPU v7x, 512 devices: a whole 4x8x8 slice. The times are simulated.
512 devices in a mesh: dp: 8 (over x, core), point: 64 (over y, z).
Axes of the slice: x: 4, y: 8, z: 8, core: 2. Of those that a mesh axis runs over, the one named last changes fastest.
Arguments:
- node_inputs_mapped: bfloat16 [8, 24576, 1024], P('dp', 'point'), as said below
- pooling_inputs: bfloat16 [8, 24576, 1024], P('dp', 'point'), may hold values from -6 to 6
- result_cotangent: bfloat16 [8, 24576, 1024], P('dp', 'point'), may hold values from -6 to 6
- partition_energy_map: bfloat16 [64, 64], replicated
- sharpness_factor: float32 [16], replicated, may hold values from 0.2 to 1
- centroid_linear_maps: float32 [64, 192], replicated, may hold values from -0.75 to 0.75
Outputs:
- layer_output: bfloat16 [8, 24576, 1024], P('dp', 'point')
- grad_mid: bfloat16 [8, 24576, 1024], P('dp', 'point')
- pooling_input_cotangent: bfloat16 [8, 24576, 1024], P('dp', 'point')
- grad_slice: float32 [64, 64], P('dp')
- grad_temp: float32 [16], P('dp')
- grad_token: float32 [64, 192], P('dp')
Inputs may be any that keep to these rules, and one draw needn't show every extreme that they name: node_inputs_mapped is of order one in most rows; a few head vectors may be much larger.
All inputs are finite; a program needn't handle non-finite values.
Results may differ from a plain program's by a relative error of at most 0.012.
The roundings to bfloat16 on the way count: a program that leaves them out, or rounds other values in their place, can miss the bound.
Values sent between devices are 32-bit elements; how exact they have to be, the bound alone decides.
A program may use at most 64 MiB of HBM per device.

v0:
```python
import jax
import jax.numpy as jnp
from jax import lax
from jax.sharding import PartitionSpec as P

epsilon = 1e-05
highest_precision = lax.Precision.HIGHEST


def partition_probability(node_channel_groups, partition_energy_map, temper):
    partition_energies = jnp.einsum(
        "phd,dm->phm", node_channel_groups, partition_energy_map, preferred_element_type=jnp.float32
    )
    partition_denominator = partition_energies / temper[None, :, None]
    return (partition_denominator, jax.nn.softmax(partition_denominator, axis=-1))


def local_pool(partition_assignment, feature_per_head):
    pooled_features = jnp.einsum(
        "onw,onf->nwf",
        partition_assignment.astype(jnp.bfloat16),
        feature_per_head,
        preferred_element_type=jnp.float32,
    )
    return (pooled_features, jnp.sum(partition_assignment, axis=0))


def per_device(
    node_inputs_mapped,
    pooling_inputs,
    result_cotangent,
    partition_energy_map,
    sharpness_factor,
    centroid_linear_maps,
):
    tally_number = node_inputs_mapped.shape[1]
    channel_groups_divide = sharpness_factor.shape[0]
    head_size = partition_energy_map.shape[0]
    node_channel_groups = node_inputs_mapped[0].reshape(
        tally_number, channel_groups_divide, head_size
    )
    feature_per_head = pooling_inputs[0].reshape(tally_number, channel_groups_divide, head_size)
    gradient_per_head = result_cotangent[0].reshape(tally_number, channel_groups_divide, head_size)
    mixed_gradient = None
    partition_denominator, partition_assignment = partition_probability(
        node_channel_groups, partition_energy_map, sharpness_factor
    )
    pooled_features, mass = local_pool(partition_assignment, feature_per_head)
    pooled_features, mass = lax.psum((pooled_features, mass), "point")
    slice_bias = partition_assignment.astype(jnp.bfloat16)
    inverse = 1.0 / (mass + epsilon)
    slice_token = pooled_features * inverse[..., None]
    projection = jnp.einsum(
        "ugb,bp->ugp", slice_token, centroid_linear_maps, precision=highest_precision
    )
    query_tokens = projection[..., :head_size]
    key_transposed = projection[..., head_size : 2 * head_size]
    value_tokens = projection[..., 2 * head_size :]
    score_scale = head_size ** (-0.5)
    attention_score = (
        jnp.einsum("sfv,siv->sfi", query_tokens, key_transposed, precision=highest_precision)
        * score_scale
    )
    attention_probs = jax.nn.softmax(attention_score, axis=-1)
    mixed_tokens = jnp.einsum(
        "lpx,lxw->lpw", attention_probs, value_tokens, precision=highest_precision
    )
    mixed_tokens_batch = mixed_tokens.astype(jnp.bfloat16)
    layer_output = jnp.einsum(
        "zfi,fil->zfl", slice_bias, mixed_tokens_batch, preferred_element_type=jnp.float32
    ).astype(jnp.bfloat16)
    mixed_gradient = jnp.einsum(
        "onw,onf->nwf", slice_bias, gradient_per_head, preferred_element_type=jnp.float32
    )
    mixed_gradient = lax.psum(mixed_gradient, "point")
    slice_gradient_1 = jnp.einsum(
        "zgu,glu->zgl", gradient_per_head, mixed_tokens_batch, preferred_element_type=jnp.float32
    )
    attention_probs_gradient = jnp.einsum(
        "sfv,siv->sfi", mixed_gradient, value_tokens, precision=highest_precision
    )
    value_gradient = jnp.einsum(
        "voi,voj->vij", attention_probs, mixed_gradient, precision=highest_precision
    )
    score_gradient = (
        attention_probs
        * (
            attention_probs_gradient
            - jnp.sum(attention_probs * attention_probs_gradient, axis=-1, keepdims=True)
        )
        * score_scale
    )
    query_gradient = jnp.einsum(
        "lpx,lxw->lpw", score_gradient, key_transposed, precision=highest_precision
    )
    key_gradient = jnp.einsum(
        "voi,voj->vij", score_gradient, query_tokens, precision=highest_precision
    )
    projection_gradient = jnp.concatenate([query_gradient, key_gradient, value_gradient], axis=-1)
    centroid_cotangent_entries = jnp.einsum(
        "qtj,qtx->jx", slice_token, projection_gradient, precision=highest_precision
    )
    token_gradient = jnp.einsum(
        "wfi,ki->wfk", projection_gradient, centroid_linear_maps, precision=highest_precision
    )
    grad_pool = token_gradient * inverse[..., None]
    mass_gradient = -jnp.sum(token_gradient * slice_token, axis=-1) * inverse
    pooled_batch_gradient = grad_pool.astype(jnp.bfloat16)
    pooling_input_cotangent = jnp.einsum(
        "zfi,fil->zfl", slice_bias, pooled_batch_gradient, preferred_element_type=jnp.float32
    ).astype(jnp.bfloat16)
    slice_gradient_sum = (
        slice_gradient_1
        + jnp.einsum(
            "zgu,glu->zgl",
            feature_per_head,
            pooled_batch_gradient,
            preferred_element_type=jnp.float32,
        )
        + mass_gradient[None]
    )
    denominator_cotangent = partition_assignment * (
        slice_gradient_sum
        - jnp.sum(partition_assignment * slice_gradient_sum, axis=-1, keepdims=True)
    )
    assignment_cotangent = denominator_cotangent / sharpness_factor[None, :, None]
    sharpness_cotangent_entries = (
        -jnp.sum(denominator_cotangent * partition_denominator, axis=(0, 2)) / sharpness_factor
    )
    grad_logit_b = assignment_cotangent.astype(jnp.bfloat16)
    grad_mid = jnp.einsum(
        "phm,dm->phd", grad_logit_b, partition_energy_map, preferred_element_type=jnp.float32
    ).astype(jnp.bfloat16)
    partition_cotangent_local = jnp.einsum(
        "phd,phm->dm", node_channel_groups, grad_logit_b, preferred_element_type=jnp.float32
    )
    surface_partition, surface_warmth = lax.psum(
        (partition_cotangent_local, sharpness_cotangent_entries), "point"
    )
    grad_slice, grad_temp, grad_token = (
        lax.psum_scatter(surface_partition, "dp", scatter_dimension=0, tiled=True),
        lax.psum_scatter(surface_warmth, "dp", scatter_dimension=0, tiled=True),
        lax.psum_scatter(centroid_cotangent_entries, "dp", scatter_dimension=0, tiled=True),
    )
    width = channel_groups_divide * head_size
    return (
        layer_output.reshape(1, tally_number, width),
        grad_mid.reshape(1, tally_number, width),
        pooling_input_cotangent.reshape(1, tally_number, width),
        grad_slice,
        grad_temp,
        grad_token,
    )


def solution(mesh):
    in_specs = (
        P("dp", "point", None),
        P("dp", "point", None),
        P("dp", "point", None),
        P(),
        P(),
        P(),
    )
    out_specs = (
        P("dp", "point", None),
        P("dp", "point", None),
        P("dp", "point", None),
        P("dp", None),
        P("dp"),
        P("dp", None),
    )
    return jax.shard_map(
        per_device, mesh=mesh, in_specs=in_specs, out_specs=out_specs, check_vma=False
    )
```

profile of v0, /device:TPU:32, one launch (start us, length us, event | category | flops | bytes accessed | tf_op | source)
XLA Modules:
  0.0 510.8 jit_solution(10793659170990280373)
XLA Ops:
  7.2 1.6 copy.45
  9.2 1.5 copy.50
  10.7 1.8 fusion.40
  12.5 1.6 fusion.38
  14.1 1.2 fusion.44
  15.3 1.2 fusion.46
  16.6 1.3 dynamic-slice
  19.2 149.5 %psum.36 = f32[16,64]{1,0:T(8,128)S(1)} all-reduce(f32[16,64]{1,0:T(8,128)S(1)} %get-tuple-element.30), channel_id=1, replica_groups=mesh['dp'=8,'point'=64] {'point'}, use_global_device_ids=true, to_apply=%region_4.0 | all-reduce | flops 1024 | bytes 8192 | tf_op jit(solution)/shard_map/psum | solution.py:49
  168.7 1.6 convolution_divide_fusion
  170.3 9.4 %all-reduce.7.cloned.1.call-done = (f32[16,64,64]{2,1,0:T(8,128)}, f32[16,64,64]{2,1,0:T(8,128)}) async-done(((f32[16,64,64]{2,1,0:T(8,128)}, f32[16,64,64]{2,1,0:T(8,128)}), (f32[16,64,64]{2,1,0:T(8,128)}, f32[16,64,64]{2,1,0:T(8,128)})) %all-reduce.7.cloned.1.call-update) | async-done | bytes 524304 | tf_op jit(solution)/shard_map/psum | solution.py:49
  179.6 2.1 fusion.19
  181.8 1.0 fusion.43
  182.9 1.0 multiply_reduce_fusion.2
  183.9 1.2 fusion.9
  186.7 0.8 copy-done.8
  187.5 2.1 convolution_bitcast_fusion
  189.6 2.6 multiply_reduce_fusion.1
  192.2 1.0 convolution_convert_fusion.3
  194.9 0.9 copy-done.9
  198.6 23.9 %all-reduce.4 = (f32[64,64]{0,1:T(8,128)S(1)}, f32[16]{0:T(128)S(1)}) all-reduce(f32[64,64]{0,1:T(8,128)S(1)} %convolution_bitcast_fusion.1, f32[16]{0:T(128)S(1)} %negate_divide_fusion), channel_id=2, replica_groups=mesh['dp'=8,'point'=64] {'dp'}, use_global_device_ids=true, to_apply=%region_12.0.clone | all-reduce | flops 4112 | bytes 32896
  222.6 277.2 %all-reduce.2 = (f32[8,64]{0,1:T(8,128)S(1)}, f32[2]{0:T(128)}) all-reduce(f32[8,64]{0,1:T(8,128)S(1)} %constant_dynamic-slice_fusion, f32[2]{0:T(128)S(1)} %dynamic-slice.3), channel_id=1, replica_groups=mesh['dp'=8,'point'=64] {'point'}, use_global_device_ids=true, to_apply=%region_11.0 | all-reduce | flops 514 | bytes 4112 | tf_op jit(solution)/shard_map/psum | solution.py:137
  500.5 1.2 copy.58
  501.7 1.2 copy.57
  502.8 1.2 copy.56
  (50 shorter events, 7.3 us)
Async XLA Ops:
  7.2 172.5 %copy-start = (f32[64,192]{1,0:T(8,128)S(1)}, f32[64,192]{1,0:T(8,128)}, u32[]{:S(2)}) copy-start(f32[64,192]{1,0:T(8,128)} %param.11) | copy-start | bytes 147460
  7.2 1.6 copy-start.10
  7.2 172.4 %all-reduce.7.cloned.1.call-start = ((), (), s32[]{:S(2)}) async-start(), calls=%async_computation.2 | async-start | bytes 2097152 | tf_op jit(solution)/shard_map/psum | solution.py:49
  8.8 159.9 %copy-start.4 = (bf16[1,384,1024]{1,2,0:T(8,128)(2,1)}, bf16[1,384,1024]{1,2,0:T(8,128)(2,1)S(1)}, u32[]{:S(2)}) copy-start(bf16[1,384,1024]{1,2,0:T(8,128)(2,1)S(1)} %copy.45) | copy-start | bytes 2359300
  8.8 1.9 copy-start.11
  8.8 1.9 copy-start.13
  16.6 487.4 %reduce-scatter.3.cloned.1.call-start = ((), (), s32[]{:S(2)}) async-start(), calls=%async_computation.1 | async-start | bytes 73728 | tf_op jit(solution)/shard_map/reduce_scatter | solution.py:143
  179.6 3.3 copy-start.12
  181.8 3.3 copy-start.2
  185.1 1.5 copy-start.6
  185.9 0.8 copy-start.7
  185.9 1.6 copy-start.1
  186.7 0.8 copy-start.8
  189.6 2.6 copy-start.3
  194.4 1.4 copy-start.9
  194.4 1.9 copy-start.14
  196.3 1.1 copy-start.5
Sparse Core Ops, SparseCore 0:
  16.7 162.8 all-reduce.6
  198.7 33.7 reduce-scatter.2
where the time goes:
time: 511 us
  blocking collectives  451 us (88%)
  matrix products  20.9 us (4%)
  between operations  15.6 us (3%)
  local copies, waits for them, and re-layouts  11.7 us (2%)
  waiting for transfers between devices  9.4 us (2%)
    psum x1, blocking collectives, per_device(): lax.psum((partition_cotangent_local, sharpness_cotangent_entries), 'point')  277 us
    psum x1, blocking collectives, per_device(): pooled_features, mass = lax.psum((pooled_features, mass), 'point')  149 us
    unnamed x1, blocking collectives  23.9 us
    unnamed x40, local copies, waits for them, and re-layouts  11.7 us
  transfers between devices with their start and end apart: 2, of which 1 were waited for; matrix products, arithmetic and copies ran while one was open for 1% of the time, Pallas kernels for 0%

commit v1 on v0

v1 whole, which is shorter than its diff:
```python
import functools

import jax
import jax.numpy as jnp
from jax import lax
from jax.experimental import pallas as pl
from jax.experimental.pallas import tpu as pltpu
from jax.sharding import PartitionSpec as P

epsilon = 1e-05
f32 = jnp.float32
bf16 = jnp.bfloat16
W = 64
Q = 4
QW = Q * W
NN = (((1,), (0,)), ((), ()))
NT = (((1,), (1,)), ((), ()))


def bdot(a, b, dims=NN):
    return lax.dot_general(a, b, dims, preferred_element_type=f32)


def hdot(a, b, dims=NN):
    return lax.dot_general(
        a, b, dims, preferred_element_type=f32, precision=lax.Precision.HIGHEST
    )


def swap_halves(x):
    return pltpu.roll(x, W, 1)


def kernel(
    N,
    ND,
    H,
    node_h,
    pool_h,
    cot_h,
    w_ref,
    sharp_ref,
    maps_ref,
    lo_ref,
    gm_ref,
    pc_ref,
    gs_ref,
    gt_ref,
    gk_ref,
    node,
    pool,
    cot,
    zed,
    sl,
    slt,
    slb,
    glt,
    bt,
    mbs,
    gbs,
    send1,
    recv1,
    send2,
    recv2,
    tok,
    res,
    acc,
    tpart,
    tgrad,
    fin,
    tred,
    fred,
    in_sem,
    s1,
    r1,
    s2,
    r2,
    sg,
    rg,
    s3,
    r3,
    st,
    rt,
    sf,
    rf,
):
    QN = H // Q
    R2 = W // N
    R = W // ND
    PTS = node.shape[0]
    point = lax.axis_index("point")
    me_d = lax.axis_index("dp")
    me_y = point // N
    me_z = point % N

    def first(f):
        return jnp.where(f == 0, me_y, me_z) if not isinstance(f, int) else (me_y, me_z)[f]

    def second(f):
        return jnp.where(f == 0, me_z, me_y) if not isinstance(f, int) else (me_z, me_y)[f]

    def place(f, i, j):
        if isinstance(f, int):
            return i * N + j if f == 0 else j * N + i
        return jnp.where(f == 0, i * N + j, j * N + i)

    def rcopy(src, dst, ssem, rsem, **dev):
        return pltpu.make_async_remote_copy(
            src_ref=src,
            dst_ref=dst,
            send_sem=ssem,
            recv_sem=rsem,
            device_id=dev,
            device_id_type=pl.DeviceIdType.MESH,
        )

    barrier = pltpu.get_barrier_semaphore()
    for k in range(1, N):
        for dev in (place(0, (me_y + k) % N, me_z), place(0, me_y, (me_z + k) % N)):
            pl.semaphore_signal(
                barrier, inc=1, device_id={"point": dev}, device_id_type=pl.DeviceIdType.MESH
            )
    for k in range(1, ND):
        pl.semaphore_signal(
            barrier,
            inc=1,
            device_id={"dp": (me_d + k) % ND},
            device_id_type=pl.DeviceIdType.MESH,
        )

    def order(t):
        return (t % 2) * (QN // 2) + t // 2 if QN > 1 else t

    def fetch(q):
        lanes = pl.ds(pl.multiple_of(q * QW, QW), QW)
        return [
            pltpu.make_async_copy(s.at[0, :, lanes], d.at[:, lanes], in_sem.at[n, q])
            for n, (s, d) in enumerate(((node_h, node), (pool_h, pool), (cot_h, cot)))
        ]

    for t in range(QN):
        for c in fetch(order(t)):
            c.start()

    w4 = jnp.concatenate([w_ref[...].astype(f32)] * Q, axis=0)
    w4 = jnp.concatenate([w4] * Q, axis=1)
    row = lax.broadcasted_iota(jnp.int32, (QW, QW), 0)
    col = lax.broadcasted_iota(jnp.int32, (QW, QW), 1)
    w4 = jnp.where(row // W == col // W, w4, 0.0)
    bt[...] = w4.T.astype(bf16)
    lane = lax.broadcasted_iota(jnp.int32, (W, 2 * W), 1)
    low = lane < W
    low8 = low[:8]

    def inv_sharp(h, width):
        return 1.0 / jnp.full((1, width), sharp_ref[h], f32)

    def rows_of(q, i=0, n=QW):
        return pl.ds(pl.multiple_of(q * QW + i * W, W), n)

    def lanes_of(q):
        return pl.ds(pl.multiple_of(q * QW, QW), QW)

    def phase1(h):
        f, i = h // N, h % N
        return rcopy(
            send1.at[h],
            recv1.at[f, first(f)],
            s1.at[h],
            r1.at[f, first(f)],
            point=place(f, i, second(f)),
        )

    def forward(t, carry):
        q = order(t)
        for c in fetch(q):
            c.wait()
        z = bdot(bt[...], node[:, lanes_of(q)], NT)
        low_parts = []
        for i in range(Q):
            zh = z[i * W : (i + 1) * W] * inv_sharp(q * Q + i, PTS)
            e = jnp.exp(zh - jnp.max(zh, axis=0, keepdims=True))
            s = e * (1.0 / jnp.sum(e, axis=0, keepdims=True))
            sb = s.astype(bf16)
            zed[rows_of(q, i, W), :] = zh
            sl[rows_of(q, i, W), :] = s
            slt[rows_of(q, i, W), :] = sb
            low_parts.append((s - sb.astype(f32)).astype(bf16))
        sq = slt[rows_of(q), :]
        ones = jnp.ones((8, PTS), bf16)
        mass = bdot(ones, sq, NT) + bdot(ones, jnp.concatenate(low_parts, axis=0), NT)
        pooled = bdot(sq, pool[:, lanes_of(q)])
        gmixed = bdot(sq, cot[:, lanes_of(q)])
        for i in range(Q):
            r, c = slice(i * W, (i + 1) * W), slice(i // 2 * 2 * W, (i // 2 + 1) * 2 * W)
            a, b, m = pooled[r, c], gmixed[r, c], mass[:, c]
            if i % 2 == 0:
                b = swap_halves(b)
            else:
                a, m = swap_halves(a), swap_halves(m)
            send1[q * Q + i, :W, :] = jnp.where(low, a, b)
            send1[q * Q + i, W:, :] = m

        @pl.when(t == 0)
        def _():
            pl.semaphore_wait(barrier, 2 * (N - 1) + ND - 1)

        for i in range(Q):
            h = q * Q + i

            @pl.when(h % N != first(h // N))
            def _():
                phase1(h).start()

        return carry

    lax.fori_loop(0, QN, forward, 0)

    def flip(q):
        slb[:, lanes_of(q)] = slt[rows_of(q), :].T

    for q in range(QN):
        flip(q)

    def phase2(f, j):
        return rcopy(
            send2.at[f, j],
            recv2.at[f, second(f)],
            s2.at[f, j],
            r2.at[f, second(f)],
            point=place(f, first(f), j),
        )

    for f in range(2):
        recv1[f, first(f)] = send1[f * N + first(f)]
        for k in range(1, N):
            i = (first(f) + k) % N
            rcopy(
                send1.at[0], recv1.at[f, i], s1.at[0], r1.at[f, i], point=place(f, i, second(f))
            ).wait_recv()
        part = recv1[f, 0]
        for i in range(1, N):
            part = part + recv1[f, i]
        for j in range(N):
            send2[f, j, :R2, :] = part[j * R2 : (j + 1) * R2]
            send2[f, j, R2:, :] = part[W:]
        for k in range(1, N):
            phase2(f, (second(f) + k) % N).start()
        recv2[f, second(f)] = send2[f, second(f)]

    def gather2(f, j):
        mine = tok.at[f, pl.ds(pl.multiple_of(second(f) * R2, R2), R2)]
        return rcopy(
            mine, mine, sg.at[f, j], rg.at[f, second(f)], point=place(f, first(f), j)
        )

    masses = []
    for f in range(2):
        for k in range(1, N):
            j = (second(f) + k) % N
            rcopy(
                send2.at[f, j], recv2.at[f, j], s2.at[f, j], r2.at[f, j], point=place(f, first(f), j)
            ).wait_recv()
        total = recv2[f, 0]
        for j in range(1, N):
            total = total + recv2[f, j]
        tok[f, pl.ds(pl.multiple_of(second(f) * R2, R2), R2), :] = total[:R2]
        for k in range(1, N):
            gather2(f, (second(f) + k) % N).start()
        masses.append(total[R2:])

    for q in range(QN):
        mbs[q] = jnp.zeros((QW, QW), bf16)
        gbs[q] = jnp.zeros((QW, QW), bf16)
    acc[...] = jnp.zeros(acc.shape, f32)

    maps = maps_ref[...]

    def phase3(f, i):
        h = f * N + first(f)
        return rcopy(
            res.at[h], res.at[h], s3.at[f, i], r3.at[h], point=place(f, i, second(f))
        )

    token_grads = []
    for f in range(2):
        for k in range(1, N):
            j = (second(f) + k) % N
            theirs = tok.at[f, pl.ds(pl.multiple_of(j * R2, R2), R2)]
            rcopy(
                theirs, theirs, sg.at[f, j], rg.at[f, j], point=place(f, first(f), j)
            ).wait_recv()
    for f in range(2):
        both = tok[f]
        inverse = (1.0 / (masses[f] + epsilon)).T[:W, :1]
        t = both[:, :W] * inverse
        gmix = swap_halves(both)[:, :W]
        proj = hdot(t, maps)
        query, key, value = proj[:, :W], swap_halves(proj[:, : 2 * W])[:, :W], proj[:, 2 * W :]
        score = hdot(query, key, NT) * W**-0.5
        e = jnp.exp(score - jnp.max(score, axis=1, keepdims=True))
        attn = e / jnp.sum(e, axis=1, keepdims=True)
        mixed = hdot(attn, value)
        gattn = hdot(gmix, value, NT)
        gvalue = hdot(attn.T, gmix)
        gscore = attn * (gattn - jnp.sum(attn * gattn, axis=1, keepdims=True)) * W**-0.5
        gquery = hdot(gscore, key)
        gkey = hdot(gscore.T, query)
        gproj = jnp.concatenate([gquery, gkey, gvalue], axis=1)
        gtok = hdot(gproj, maps, NT)
        gpool = gtok * inverse
        gmass = hdot(jnp.ones((8, W), f32), -(gtok * t) * inverse, NT)
        h = f * N + first(f)
        res[h, :W, :] = jnp.concatenate(
            [mixed.astype(bf16).astype(f32), gpool.astype(bf16).astype(f32)], axis=1
        )
        zero8 = jnp.zeros((8, W), f32)
        res[h, W:, :] = jnp.where(
            (jnp.zeros((8, 2 * W), jnp.int32) + h) % 2 == 0,
            jnp.concatenate([gmass, zero8], axis=1),
            jnp.concatenate([zero8, gmass], axis=1),
        )
        for k in range(1, N):
            phase3(f, (first(f) + k) % N).start()
        token_grads.append(hdot(t.T, gproj))

    def all_of(buf, ssem, rsem):
        axes = ((me_d, ND), (me_z, N), (me_y, N))

        def dev(stage, k):
            if stage == 0:
                return {"dp": k}
            return {"point": place(0, me_y, k) if stage == 1 else place(0, k, me_z)}

        def copy(stage, k, src):
            me = axes[stage][0]
            return rcopy(
                src, buf.at[stage, me], ssem.at[stage, k], rsem.at[stage, me], **dev(stage, k)
            )

        def send(stage, source):
            me, n = axes[stage]
            for k in range(1, n):
                k = (me + k) % n
                copy(stage, k, source(k)).start()

        def receive(stage):
            me, n = axes[stage]
            for k in range(1, n):
                k = (me + k) % n
                rcopy(
                    buf.at[stage, k],
                    buf.at[stage, k],
                    ssem.at[stage, k],
                    rsem.at[stage, k],
                    **dev(stage, k),
                ).wait_recv()
            total = buf[stage, 0]
            for k in range(1, n):
                total = total + buf[stage, k]
            return total

        def begin(source):
            buf[0, me_d] = source[me_d]
            send(0, lambda k: source.at[k])

        def onward(stage):
            total = receive(stage - 1)
            me = axes[stage][0]
            buf[stage, me] = total
            send(stage, lambda k: buf.at[stage, me])

        def finish():
            return receive(2)

        def drain():
            for stage in range(3):
                me, n = axes[stage]
                for k in range(1, n):
                    k = (me + k) % n
                    copy(stage, k, buf.at[stage, me]).wait_send()

        return begin, onward, finish, drain

    t_begin, t_onward, t_finish, t_drain = all_of(tred, st, rt)
    f_begin, f_onward, f_finish, f_drain = all_of(fred, sf, rf)

    tg = (token_grads[0] + token_grads[1]) * (1.0 / N)
    tg = jnp.concatenate([tg, jnp.zeros((W, W), f32)], axis=1)
    for d in range(ND):
        tgrad[d] = tg[d * R : (d + 1) * R]
    t_begin(tgrad)

    def backward(t, carry):
        q = order(t)
        for i in range(Q):
            h = q * Q + i
            f = h // N

            @pl.when(h % N != first(f))
            def _():
                rcopy(
                    res.at[h], res.at[h], s3.at[0, 0], r3.at[h], point=place(f, h % N, second(f))
                ).wait_recv()

        cols = []
        for i in range(Q):
            c = slice(i // 2 * 2 * W, (i // 2 + 1) * 2 * W)
            r = slice(i * W, (i + 1) * W)
            both = res[q * Q + i, :W, :]
            other = swap_halves(both)
            m, g = (both, other) if i % 2 == 0 else (other, both)
            keep = low if i % 2 == 0 else ~low
            mbs[q, r, c] = jnp.where(keep, m, 0.0).astype(bf16)
            gbs[q, r, c] = jnp.where(keep, g, 0.0).astype(bf16)
            if i % 2 == 0:
                cols.append((res[q * Q + i, W:, :] + res[q * Q + i + 1, W:, :]).T[:, :1])
        gq = bdot(mbs[q], cot[:, lanes_of(q)], NT) + bdot(gbs[q], pool[:, lanes_of(q)], NT)
        for i in range(Q):
            h = q * Q + i
            s = sl[rows_of(q, i, W), :]
            g = gq[i * W : (i + 1) * W] + cols[i // 2][i % 2 * W : (i % 2 + 1) * W]
            sg_ = s * g
            gz = sg_ - s * jnp.sum(sg_, axis=0, keepdims=True)
            glt[rows_of(q, i, W), :] = (gz * inv_sharp(h, PTS)).astype(bf16)
            tz = gz * zed[rows_of(q, i, W), :]
            tpart[h] = jnp.sum(tz.reshape(W // 8, 8, PTS), axis=0)
        gs = bdot(glt[rows_of(q), :], node[:, lanes_of(q)])
        for i in range(Q):
            c = slice(i // 2 * 2 * W, (i // 2 + 1) * 2 * W)
            acc[i % 2] += gs[i * W : (i + 1) * W, c]
        return carry

    lax.fori_loop(0, QN, backward, 0)
    t_onward(1)

    gst = jnp.where(low, acc[0] + swap_halves(acc[1]), 0.0)
    gst = jnp.concatenate([gst, jnp.zeros((W, 2 * W), f32)], axis=0).T[:W]
    temps = []
    for h in range(H):
        v = jnp.sum(jnp.sum(tpart[h], axis=0, keepdims=True), axis=1, keepdims=True)
        temps.append(-v * inv_sharp(h, 1))
    each = H // ND
    wide = lax.broadcasted_iota(jnp.int32, (R, 2 * W), 1)
    for d in range(ND):
        v = gst[d * R : (d + 1) * R]
        for n in range(each):
            v = v + jnp.where(wide == W + n, temps[d * each + n], 0.0)
        fin[d] = v
    f_begin(fin)

    def outputs(q):
        lanes = lanes_of(q)
        gl = glt[rows_of(q), :].T
        gm_ref[0, :, lanes] = bdot(gl, bt[...]).astype(bf16)
        lo_ref[0, :, lanes] = bdot(slb[:, lanes], mbs[q]).astype(bf16)
        pc_ref[0, :, lanes] = bdot(slb[:, lanes], gbs[q]).astype(bf16)

    t_onward(2)
    f_onward(1)
    for q in range(0, QN // 2):
        outputs(q)
    f_onward(2)
    for q in range(QN // 2, QN):
        outputs(q)
    gk_ref[...] = t_finish()[:, : 3 * W]
    last = f_finish()
    gs_ref[...] = last[:, :W]
    for n in range(each):
        gt_ref[n] = jnp.sum(jnp.where(wide[:1] == W + n, last[:1], 0.0))

    for h in range(H):
        f, i = h // N, h % N

        @pl.when(i != first(f))
        def _():
            phase1(h).wait_send()

    for f in range(2):
        for k in range(1, N):
            phase2(f, (second(f) + k) % N).wait_send()
            gather2(f, (second(f) + k) % N).wait_send()
            phase3(f, (first(f) + k) % N).wait_send()
    t_drain()
    f_drain()


def per_device(N, ND, node, pool, cot, w, sharp, maps):
    _, pts, width = node.shape
    H = sharp.shape[0]
    QN = H // Q
    R2 = W // N
    R = W // ND
    vmem = pl.BlockSpec(memory_space=pltpu.VMEM)
    smem = pl.BlockSpec(memory_space=pltpu.SMEM)
    hbm = pl.BlockSpec(memory_space=pltpu.HBM)
    big = jax.ShapeDtypeStruct((1, pts, width), bf16)
    dma = pltpu.SemaphoreType.DMA
    return pl.pallas_call(
        functools.partial(kernel, N, ND, H),
        out_shape=(
            big,
            big,
            big,
            jax.ShapeDtypeStruct((R, W), f32),
            jax.ShapeDtypeStruct((H // ND,), f32),
            jax.ShapeDtypeStruct((R, 3 * W), f32),
        ),
        in_specs=[hbm, hbm, hbm, vmem, smem, vmem],
        out_specs=(vmem, vmem, vmem, vmem, smem, vmem),
        scratch_shapes=[
            pltpu.VMEM((pts, width), bf16),
            pltpu.VMEM((pts, width), bf16),
            pltpu.VMEM((pts, width), bf16),
            pltpu.VMEM((width, pts), f32),
            pltpu.VMEM((width, pts), f32),
            pltpu.VMEM((width, pts), bf16),
            pltpu.VMEM((pts, width), bf16),
            pltpu.VMEM((width, pts), bf16),
            pltpu.VMEM((QW, QW), bf16),
            pltpu.VMEM((QN, QW, QW), bf16),
            pltpu.VMEM((QN, QW, QW), bf16),
            pltpu.VMEM((H, W + 8, 2 * W), f32),
            pltpu.VMEM((2, N, W + 8, 2 * W), f32),
            pltpu.VMEM((2, N, R2 + 8, 2 * W), f32),
            pltpu.VMEM((2, N, R2 + 8, 2 * W), f32),
            pltpu.VMEM((2, W, 2 * W), f32),
            pltpu.VMEM((H, W + 8, 2 * W), f32),
            pltpu.VMEM((2, W, 2 * W), f32),
            pltpu.VMEM((H, 8, pts), f32),
            pltpu.VMEM((ND, R, 4 * W), f32),
            pltpu.VMEM((ND, R, 2 * W), f32),
            pltpu.VMEM((3, max(N, ND), R, 4 * W), f32),
            pltpu.VMEM((3, max(N, ND), R, 2 * W), f32),
            dma((3, QN)),
            dma((H,)),
            dma((2, N)),
            dma((2, N)),
            dma((2, N)),
            dma((2, N)),
            dma((2, N)),
            dma((2, N)),
            dma((H,)),
            dma((3, max(N, ND))),
            dma((3, max(N, ND))),
            dma((3, max(N, ND))),
            dma((3, max(N, ND))),
        ],
        compiler_params=pltpu.CompilerParams(
            collective_id=0, has_side_effects=True, vmem_limit_bytes=32 * 1024 * 1024
        ),
    )(node, pool, cot, w, sharp, maps)


def solution(mesh):
    N = int(round(mesh.shape["point"] ** 0.5))
    ND = mesh.shape["dp"]
    big = P("dp", "point", None)
    return jax.shard_map(
        functools.partial(per_device, N, ND),
        mesh=mesh,
        in_specs=(big, big, big, P(), P(), P()),
        out_specs=(big, big, big, P("dp", None), P("dp"), P("dp", None)),
        check_vma=False,
    )
```

time: 511 us -> 76.3 us (0.15)
  the two profiles are of different devices: /device:TPU:32 before, /device:TPU:6 now
where the time goes in v1:
time: 76.3 us; the launch traced here: 75.9 us
  Pallas kernels  65.3 us (86%)
  local copies, waits for them, and re-layouts  9.94 us (13%)
    pallas_call x1, Pallas kernels, per_device(): pl.pallas_call(functools.partial(kernel, N, ND, H), out_shape=(big, big,...  65.3 us
    unnamed x18, local copies, waits for them, and re-layouts  9.94 us

profile of v1, /device:TPU:6, one launch (start us, length us, event | category | flops | bytes accessed | tf_op | source)
XLA Modules:
  0.0 75.9 jit_solution(3682811143939116152)
XLA Ops:
  0.6 0.0 copy-start
  0.6 1.1 %copy-done = bf16[1,384,1024]{2,1,0:T(8,128)(2,1)S(1)} copy-done((bf16[1,384,1024]{2,1,0:T(8,128)(2,1)S(1)}, bf16[1,384,1024]{2,1,0:T(8,128)(2,1)}, u32[]{:S(2)}) %copy-start) | copy-done | bytes 786456
  1.8 0.0 copy-start.1
  1.8 1.1 %copy-done.1 = bf16[1,384,1024]{2,1,0:T(8,128)(2,1)S(1)} copy-done((bf16[1,384,1024]{2,1,0:T(8,128)(2,1)S(1)}, bf16[1,384,1024]{2,1,0:T(8,128)(2,1)}, u32[]{:S(2)}) %copy-start.1) | copy-done | bytes 786456
  2.9 0.0 copy-start.2
  2.9 1.1 %copy-done.2 = bf16[1,384,1024]{2,1,0:T(8,128)(2,1)S(1)} copy-done((bf16[1,384,1024]{2,1,0:T(8,128)(2,1)S(1)}, bf16[1,384,1024]{2,1,0:T(8,128)(2,1)}, u32[]{:S(2)}) %copy-start.2) | copy-done | bytes 786456
  4.0 0.0 copy-start.3
  4.0 0.8 %copy-done.3 = f32[64,192]{1,0:T(8,128)S(1)} copy-done((f32[64,192]{1,0:T(8,128)S(1)}, f32[64,192]{1,0:T(8,128)}, u32[]{:S(2)}) %copy-start.3) | copy-done | bytes 49176
  4.9 0.0 copy-start.4
  4.9 0.7 copy-done.4
  5.6 0.0 copy-start.5
  5.6 0.7 copy-done.5
  6.2 65.3 %shard_map.109 = (bf16[1,384,1024]{2,1,0:T(8,128)(2,1)S(1)}, bf16[1,384,1024]{2,1,0:T(8,128)(2,1)S(1)}, bf16[1,384,1024]{2,1,0:T(8,128)(2,1)S(1)}, f32[8,64]{1,0...) custom-call(bf16[1,384,1024]{2,1,0:T(8,128)(2,1)S(1)} %copy-done, bf16[1,384,1024]{2,1,0:T(8,128)(2,1)S(1)} %copy-done.1, ...), custom_call_target="tpu_custom_call" | custom-call | tf_op jit(solution)/shard_map/pallas_call | solution.py:499
  71.6 0.9 %copy.18 = bf16[1,384,1024]{2,1,0:T(8,128)(2,1)} copy(bf16[1,384,1024]{2,1,0:T(8,128)(2,1)S(1)} %get-tuple-element.12) | data formatting | bytes 1572864
  72.5 0.9 %copy.19 = bf16[1,384,1024]{2,1,0:T(8,128)(2,1)} copy(bf16[1,384,1024]{2,1,0:T(8,128)(2,1)S(1)} %get-tuple-element.13) | data formatting | bytes 1572864
  73.3 0.9 %copy.20 = bf16[1,384,1024]{2,1,0:T(8,128)(2,1)} copy(bf16[1,384,1024]{2,1,0:T(8,128)(2,1)S(1)} %get-tuple-element.14) | data formatting | bytes 1572864
  74.2 0.6 copy.21
  74.8 0.5 copy.22
  75.3 0.6 copy.23
Async XLA Ops:
  0.6 1.1 %copy-start = (bf16[1,384,1024]{2,1,0:T(8,128)(2,1)S(1)}, bf16[1,384,1024]{2,1,0:T(8,128)(2,1)}, u32[]{:S(2)}) copy-start(bf16[1,384,1024]{2,1,0:T(8,128)(2,1)} %node_h.1) | copy-start | bytes 2359300
  1.8 1.1 %copy-start.1 = (bf16[1,384,1024]{2,1,0:T(8,128)(2,1)S(1)}, bf16[1,384,1024]{2,1,0:T(8,128)(2,1)}, u32[]{:S(2)}) copy-start(bf16[1,384,1024]{2,1,0:T(8,128)(2,1)} %pool_h.1) | copy-start | bytes 2359300
  2.9 1.1 %copy-start.2 = (bf16[1,384,1024]{2,1,0:T(8,128)(2,1)S(1)}, bf16[1,384,1024]{2,1,0:T(8,128)(2,1)}, u32[]{:S(2)}) copy-start(bf16[1,384,1024]{2,1,0:T(8,128)(2,1)} %cot_h.1) | copy-start | bytes 2359300
  4.0 0.8 %copy-start.3 = (f32[64,192]{1,0:T(8,128)S(1)}, f32[64,192]{1,0:T(8,128)}, u32[]{:S(2)}) copy-start(f32[64,192]{1,0:T(8,128)} %maps_ref.1) | copy-start | bytes 147460
  4.9 0.7 copy-start.4
  5.6 0.7 copy-start.5

commit v2 on v1

v2 whole, which is shorter than its diff:
```python
import functools

import jax
import jax.numpy as jnp
from jax import lax
from jax.experimental import pallas as pl
from jax.experimental.pallas import tpu as pltpu
from jax.sharding import PartitionSpec as P

epsilon = 1e-05
f32 = jnp.float32
bf16 = jnp.bfloat16
W = 64
Q = 4
QW = Q * W
VMEM_LIMIT = 40 * 1024 * 1024
NN = (((1,), (0,)), ((), ()))
NT = (((1,), (1,)), ((), ()))


def bdot(a, b, dims=NN):
    return lax.dot_general(a, b, dims, preferred_element_type=f32)


def hdot(a, b, dims=NN):
    ah, bh = a.astype(bf16), b.astype(bf16)
    al, bl = (a - ah.astype(f32)).astype(bf16), (b - bh.astype(f32)).astype(bf16)
    return bdot(ah, bh, dims) + (bdot(ah, bl, dims) + bdot(al, bh, dims))


def swap_halves(x):
    return pltpu.roll(x, W, 1)


def kernel(
    N,
    ND,
    H,
    node_h,
    pool_h,
    cot_h,
    w_h,
    sharp_h,
    maps_h,
    lo_ref,
    gm_ref,
    pc_ref,
    small_ref,
    node,
    pool,
    cot,
    w_ref,
    sharp_ref,
    maps_ref,
    zed,
    sl,
    slt,
    slb,
    glt,
    gpart,
    bt,
    mbs,
    gbs,
    send1,
    recv1,
    recv2,
    res,
    acc,
    tpart,
    tgrad,
    fin,
    tred,
    fred,
    in_sem,
    par_sem,
    s1,
    r1,
    s2,
    r2,
    s3,
    r3,
    st,
    rt,
    sf,
    rf,
):
    QN = H // Q
    W2 = W // 2
    R = W // ND
    PTS = node.shape[0]
    point = lax.axis_index("point")
    me_d = lax.axis_index("dp")
    me_y = point // N
    me_z = point % N

    def first(f):
        return jnp.where(f == 0, me_y, me_z) if not isinstance(f, int) else (me_y, me_z)[f]

    def second(f):
        return jnp.where(f == 0, me_z, me_y) if not isinstance(f, int) else (me_z, me_y)[f]

    def place(f, i, j):
        if isinstance(f, int):
            return i * N + j if f == 0 else j * N + i
        return jnp.where(f == 0, i * N + j, j * N + i)

    def rcopy(src, dst, ssem, rsem, **dev):
        return pltpu.make_async_remote_copy(
            src_ref=src,
            dst_ref=dst,
            send_sem=ssem,
            recv_sem=rsem,
            device_id=dev,
            device_id_type=pl.DeviceIdType.MESH,
        )

    def wait_bytes(like, sem):
        pltpu.make_async_copy(like, like, sem).wait()

    def order(t):
        return (t % 2) * (QN // 2) + t // 2 if QN > 1 else t

    def fetch(q):
        lanes = pl.ds(pl.multiple_of(q * QW, QW), QW)
        return [
            pltpu.make_async_copy(s.at[0, :, lanes], d.at[:, lanes], in_sem.at[n, q])
            for n, (s, d) in enumerate(((node_h, node), (pool_h, pool), (cot_h, cot)))
        ]

    params = [
        pltpu.make_async_copy(s, d, par_sem.at[n])
        for n, (s, d) in enumerate(((w_h, w_ref), (sharp_h, sharp_ref), (maps_h, maps_ref)))
    ]
    for c in params:
        c.start()
    for t in range(QN):
        for c in fetch(order(t)):
            c.start()

    barrier = pltpu.get_barrier_semaphore()
    for k in range(1, N):
        for dev in (place(0, (me_y + k) % N, me_z), place(0, me_y, (me_z + k) % N)):
            pl.semaphore_signal(
                barrier, inc=1, device_id={"point": dev}, device_id_type=pl.DeviceIdType.MESH
            )
    for k in range(1, ND):
        pl.semaphore_signal(
            barrier,
            inc=1,
            device_id={"dp": (me_d + k) % ND},
            device_id_type=pl.DeviceIdType.MESH,
        )

    for c in params:
        c.wait()
    w4 = jnp.concatenate([w_ref[...].astype(f32)] * Q, axis=0)
    w4 = jnp.concatenate([w4] * Q, axis=1)
    row = lax.broadcasted_iota(jnp.int32, (QW, QW), 0)
    col = lax.broadcasted_iota(jnp.int32, (QW, QW), 1)
    w4 = jnp.where(row // W == col // W, w4, 0.0)
    bt[...] = w4.T.astype(bf16)
    low = lax.broadcasted_iota(jnp.int32, (W, 2 * W), 1) < W
    low2 = low[:W2]

    def inv_sharp(h, width):
        return 1.0 / jnp.full((1, width), sharp_ref[h], f32)

    def rows_of(q, i=0, n=QW):
        return pl.ds(pl.multiple_of(q * QW + i * W, W), n)

    def lanes_of(q):
        return pl.ds(pl.multiple_of(q * QW, QW), QW)

    def fold(x, i):
        if i % 2 == 0:
            return jnp.where(low2, x[:W2], swap_halves(x[W2:]))
        return jnp.where(low2, swap_halves(x[:W2]), x[W2:])

    def unfold(x):
        return jnp.concatenate([x[:, :W], swap_halves(x)[:, :W]], axis=0)

    def spread(x, i):
        other = swap_halves(x)
        up, down = (x, other) if i % 2 == 0 else (other, x)
        keep = low2 if i % 2 == 0 else ~low2
        return jnp.concatenate([jnp.where(keep, up, 0.0), jnp.where(keep, down, 0.0)], axis=0)

    def column(row):
        return jnp.broadcast_to(row, (8, 2 * W)).T[:, :1]

    rows_in = (W2 + 1, W2)
    rows_out = (W2, W2 + 1)

    def phase1(s, h, f, i):
        n = pl.ds(0, rows_in[s])
        return rcopy(
            send1.at[s, h, n],
            recv1.at[s, f, first(f), n],
            s1.at[s],
            r1.at[s, f],
            point=place(f, i, second(f)),
        )

    def forward(t, carry):
        q = order(t)
        for c in fetch(q):
            c.wait()
        z = bdot(bt[...], node[:, lanes_of(q)], NT)
        sums = []
        for i in range(Q):
            zh = z[i * W : (i + 1) * W] * inv_sharp(q * Q + i, PTS)
            e = jnp.exp(zh - jnp.max(zh, axis=0, keepdims=True))
            s = e * (1.0 / jnp.sum(e, axis=0, keepdims=True))
            sb = s.astype(bf16)
            zed[rows_of(q, i, W), :] = zh
            sl[rows_of(q, i, W), :] = s
            slt[rows_of(q, i, W), :] = sb
            sums.append(sum(s[:, c : c + 2 * W] for c in range(0, PTS, 2 * W)))
        sq = slt[rows_of(q), :]
        sums = jnp.concatenate(sums, axis=0)
        top = sums.astype(bf16)
        ones = jnp.ones((8, 2 * W), bf16)
        mass = bdot(ones, top, NT) + bdot(ones, (sums - top.astype(f32)).astype(bf16), NT)
        pooled = bdot(sq, pool[:, lanes_of(q)])
        gmixed = bdot(sq, cot[:, lanes_of(q)])
        for i in range(Q):
            r, c = slice(i * W, (i + 1) * W), slice(i // 2 * 2 * W, (i // 2 + 1) * 2 * W)
            m = mass[:, c] if i % 2 == 0 else swap_halves(mass[:, c])
            send1[0, q * Q + i, :W2, :] = fold(pooled[r, c], i)
            send1[0, q * Q + i, W2:, :] = m
            send1[1, q * Q + i, :W2, :] = fold(gmixed[r, c], i)

        @pl.when(t == 0)
        def _():
            pl.semaphore_wait(barrier, 2 * (N - 1) + ND - 1)

        for s in range(2):
            for i in range(Q):
                h = q * Q + i

                @pl.when(h % N != first(h // N))
                def _():
                    phase1(s, h, h // N, h % N).start()

        return carry

    lax.fori_loop(0, QN, forward, 0)

    def flip(q):
        slb[:, lanes_of(q)] = slt[rows_of(q), :].T

    for q in range(QN):
        flip(q)

    def phase2(s, f, j):
        mine = recv2.at[s, f, second(f), pl.ds(0, rows_in[s])]
        return rcopy(
            mine, mine, s2.at[s], r2.at[s, f], point=place(f, first(f), j)
        )

    def arrived1(s, f):
        h = f * N + first(f)
        own = send1[s, h]
        recv1[s, f, first(f)] = own
        wait_bytes(recv1.at[s, f, pl.ds(0, N - 1), pl.ds(0, rows_in[s])], r1.at[s, f])
        n = rows_in[s]
        part = recv1[s, f, 0, :n, :]
        for i in range(1, N):
            part = part + recv1[s, f, i, :n, :]
        recv2[s, f, second(f), :n, :] = part
        for k in range(1, N):
            phase2(s, f, (second(f) + k) % N).start()

    def arrived2(s, f):
        n = rows_in[s]
        wait_bytes(recv2.at[s, f, pl.ds(0, N - 1), pl.ds(0, n)], r2.at[s, f])
        total = recv2[s, f, 0, :n, :]
        for j in range(1, N):
            total = total + recv2[s, f, j, :n, :]
        return total

    for s in range(2):
        for f in range(2):
            arrived1(s, f)

    for q in range(QN):
        mbs[q] = jnp.zeros((QW, QW), bf16)
        gbs[q] = jnp.zeros((QW, QW), bf16)
    acc[...] = jnp.zeros(acc.shape, f32)

    maps = maps_ref[...]

    def phase3(s, f, i):
        h = f * N + first(f)
        mine = res.at[s, h, pl.ds(0, rows_out[s])]
        return rcopy(
            mine, mine, s3.at[s], r3.at[s, f], point=place(f, i, second(f))
        )

    def send3(s, f):
        for k in range(1, N):
            phase3(s, f, (first(f) + k) % N).start()

    totals = [arrived2(0, f) for f in range(2)]
    mass = jnp.concatenate([total[W2:] for total in totals], axis=0)
    mass = jnp.concatenate([mass, jnp.ones((6, 2 * W), f32)], axis=0).T
    inverse = 1.0 / (jnp.concatenate([mass[:W, :1], mass[:W, 1:2]], axis=0) + epsilon)
    t = jnp.concatenate([unfold(total[:W2]) for total in totals], axis=0) * inverse
    proj = hdot(t, maps)
    query, key, value = proj[:, :W], swap_halves(proj[:, : 2 * W])[:, :W], proj[:, 2 * W :]
    score = hdot(query, key, NT) * W**-0.5
    row = lax.broadcasted_iota(jnp.int32, (2 * W, 2 * W), 0)
    col = lax.broadcasted_iota(jnp.int32, (2 * W, 2 * W), 1)
    score = jnp.where(row // W == col // W, score, -jnp.inf)
    e = jnp.exp(score - jnp.max(score, axis=1, keepdims=True))
    attn = e / jnp.sum(e, axis=1, keepdims=True)
    mixed = hdot(attn, value).astype(bf16).astype(f32)
    for f in range(2):
        res[0, f * N + first(f), :W2, :] = jnp.concatenate(
            [mixed[f * W : f * W + W2], mixed[f * W + W2 : (f + 1) * W]], axis=1
        )
        send3(0, f)

    gmix = jnp.concatenate([unfold(arrived2(1, f)) for f in range(2)], axis=0)
    gattn = hdot(gmix, value, NT)
    gvalue = hdot(attn.T, gmix)
    gscore = attn * (gattn - jnp.sum(attn * gattn, axis=1, keepdims=True)) * W**-0.5
    gquery = hdot(gscore, key)
    gkey = hdot(gscore.T, query)
    gproj = jnp.concatenate([gquery, gkey, gvalue], axis=1)
    gtok = hdot(gproj, maps, NT)
    gpool = (gtok * inverse).astype(bf16).astype(f32)
    gmass = hdot(jnp.ones((8, W), f32), -(gtok * t) * inverse, NT)
    for f in range(2):
        h = f * N + first(f)
        res[1, h, :W2, :] = jnp.concatenate(
            [gpool[f * W : f * W + W2], gpool[f * W + W2 : (f + 1) * W]], axis=1
        )
        here, there = (gmass, swap_halves(gmass)) if f == 0 else (swap_halves(gmass), gmass)
        even = (jnp.zeros((8, 2 * W), jnp.int32) + h) % 2 == 0
        res[1, h, W2:, :] = jnp.where(
            even, jnp.where(low[:8], here, 0.0), jnp.where(low[:8], 0.0, there)
        )
        send3(1, f)

    def all_of(buf, ssem, rsem):
        axes = ((me_d, ND), (me_z, N), (me_y, N))

        def dev(stage, k):
            if stage == 0:
                return {"dp": k}
            return {"point": place(0, me_y, k) if stage == 1 else place(0, k, me_z)}

        def copy(stage, k, src):
            me = axes[stage][0]
            return rcopy(
                src, buf.at[stage, me], ssem.at[stage], rsem.at[stage], **dev(stage, k)
            )

        def send(stage, source):
            me, n = axes[stage]
            for k in range(1, n):
                k = (me + k) % n
                copy(stage, k, source(k)).start()

        def receive(stage):
            me, n = axes[stage]
            wait_bytes(buf.at[stage, pl.ds(0, n - 1)], rsem.at[stage])
            total = buf[stage, 0]
            for k in range(1, n):
                total = total + buf[stage, k]
            return total

        def begin(source):
            buf[0, me_d] = source[me_d]
            send(0, lambda k: source.at[k])

        def onward(stage):
            total = receive(stage - 1)
            me = axes[stage][0]
            buf[stage, me] = total
            send(stage, lambda k: buf.at[stage, me])

        def finish():
            return receive(2)

        def drain():
            for stage in range(3):
                n = axes[stage][1]
                wait_bytes(buf.at[stage, pl.ds(0, n - 1)], ssem.at[stage])

        return begin, onward, finish, drain

    t_begin, t_onward, t_finish, t_drain = all_of(tred, st, rt)
    f_begin, f_onward, f_finish, f_drain = all_of(fred, sf, rf)

    tg = hdot(t.T, gproj) * (1.0 / N)
    tg = jnp.concatenate([tg, jnp.zeros((W, W), f32)], axis=1)
    for d in range(ND):
        tgrad[d] = tg[d * R : (d + 1) * R]
    t_begin(tgrad)

    def halves(s, body):
        for f in range(2):
            wait_bytes(res.at[s, pl.ds(0, N - 1), pl.ds(0, rows_out[s])], r3.at[s, f])
            if QN > 1:
                lax.fori_loop(f * (QN // 2), (f + 1) * (QN // 2), body, 0)
        if QN == 1:
            body(0, 0)

    def pair(i):
        return slice(i // 2 * 2 * W, (i // 2 + 1) * 2 * W)

    def with_mixed(q, carry):
        for i in range(Q):
            mbs[q, i * W : (i + 1) * W, pair(i)] = spread(res[0, q * Q + i, :W2, :], i).astype(bf16)
        gpart[rows_of(q), :] = bdot(mbs[q], cot[:, lanes_of(q)], NT)
        lo_ref[0, :, lanes_of(q)] = bdot(slb[:, lanes_of(q)], mbs[q]).astype(bf16)
        return carry

    halves(0, with_mixed)
    t_onward(1)

    def backward(q, carry):
        cols = []
        for i in range(Q):
            gbs[q, i * W : (i + 1) * W, pair(i)] = spread(res[1, q * Q + i, :W2, :], i).astype(bf16)
            if i % 2 == 0:
                cols.append(
                    column(
                        res[1, q * Q + i, W2 : W2 + 1, :] + res[1, q * Q + i + 1, W2 : W2 + 1, :]
                    )
                )
        gq = gpart[rows_of(q), :] + bdot(gbs[q], pool[:, lanes_of(q)], NT)
        for i in range(Q):
            h = q * Q + i
            s = sl[rows_of(q, i, W), :]
            g = gq[i * W : (i + 1) * W] + cols[i // 2][i % 2 * W : (i % 2 + 1) * W]
            sg = s * g
            gz = sg - s * jnp.sum(sg, axis=0, keepdims=True)
            glt[rows_of(q, i, W), :] = (gz * inv_sharp(h, PTS)).astype(bf16)
            tz = gz * zed[rows_of(q, i, W), :]
            tpart[h] = jnp.sum(tz.reshape(W // 8, 8, PTS), axis=0)
        gs = bdot(glt[rows_of(q), :], node[:, lanes_of(q)])
        for i in range(Q):
            acc[i % 2] += gs[i * W : (i + 1) * W, pair(i)]
        return carry

    halves(1, backward)

    gst = jnp.where(low, acc[0] + swap_halves(acc[1]), 0.0)
    gst = jnp.concatenate([gst, jnp.zeros((W, 2 * W), f32)], axis=0).T[:W]
    temps = []
    for h in range(H):
        v = jnp.sum(jnp.sum(tpart[h], axis=0, keepdims=True), axis=1, keepdims=True)
        temps.append(-v * inv_sharp(h, 1))
    each = H // ND
    wide = lax.broadcasted_iota(jnp.int32, (R, 2 * W), 1)
    for d in range(ND):
        v = gst[d * R : (d + 1) * R]
        for n in range(each):
            v = v + jnp.where(wide == W + n, temps[d * each + n], 0.0)
        fin[d] = v
    f_begin(fin)

    def outputs(q):
        gl = glt[rows_of(q), :].T
        gm_ref[0, :, lanes_of(q)] = bdot(gl, bt[...]).astype(bf16)
        pc_ref[0, :, lanes_of(q)] = bdot(slb[:, lanes_of(q)], gbs[q]).astype(bf16)

    t_onward(2)
    for q in range(QN):
        outputs(q)
    f_onward(1)
    for s in range(2):
        wait_bytes(send1.at[s, pl.ds(0, 2 * N - 2), pl.ds(0, rows_in[s])], s1.at[s])
        wait_bytes(recv2.at[s, :, pl.ds(0, N - 1), pl.ds(0, rows_in[s])], s2.at[s])
        wait_bytes(res.at[s, pl.ds(0, 2 * N - 2), pl.ds(0, rows_out[s])], s3.at[s])
    f_onward(2)
    small_ref[:, 2 * W :] = t_finish()
    t_drain()
    small_ref[:, : 2 * W] = f_finish()
    f_drain()


def finish_kernel(
    each,
    lo_i,
    gm_i,
    pc_i,
    small,
    lo_h,
    gm_h,
    pc_h,
    gs_h,
    gt_h,
    gk_h,
    gs,
    gk,
    gt,
    sem,
):
    pairs = [(lo_i, lo_h), (gm_i, gm_h), (pc_i, pc_h), (gs, gs_h), (gk, gk_h), (gt, gt_h)]
    copies = [pltpu.make_async_copy(s, d, sem.at[n]) for n, (s, d) in enumerate(pairs)]
    for c in copies[:3]:
        c.start()
    gs[...] = small[:, :W]
    gk[...] = small[:, 2 * W : 5 * W]
    spot = lax.broadcasted_iota(jnp.int32, (1, 2 * W), 1)
    for n in range(each):
        gt[n] = jnp.sum(jnp.where(spot == W + n, small[:1, : 2 * W], 0.0))
    for c in copies[3:]:
        c.start()
    for c in copies:
        c.wait()


def per_device(N, ND, node, pool, cot, w, sharp, maps):
    _, pts, width = node.shape
    H = sharp.shape[0]
    QN = H // Q
    W2 = W // 2
    R = W // ND
    any_ = pl.BlockSpec(memory_space=pl.ANY)
    vmem = pl.BlockSpec(memory_space=pltpu.VMEM)
    big = jax.ShapeDtypeStruct((1, pts, width), bf16)
    dma = pltpu.SemaphoreType.DMA
    node, pool, cot, w, sharp, maps = (
        pltpu.with_memory_space_constraint(a, pltpu.HBM) for a in (node, pool, cot, w, sharp, maps)
    )
    lo, gm, pc, small = pl.pallas_call(
        functools.partial(kernel, N, ND, H),
        out_shape=(big, big, big, jax.ShapeDtypeStruct((R, 6 * W), f32)),
        in_specs=[any_] * 6,
        out_specs=[vmem] * 4,
        scratch_shapes=[
            pltpu.VMEM((pts, width), bf16),
            pltpu.VMEM((pts, width), bf16),
            pltpu.VMEM((pts, width), bf16),
            pltpu.VMEM((W, W), bf16),
            pltpu.SMEM((H,), f32),
            pltpu.VMEM((W, 3 * W), f32),
            pltpu.VMEM((width, pts), f32),
            pltpu.VMEM((width, pts), f32),
            pltpu.VMEM((width, pts), bf16),
            pltpu.VMEM((pts, width), bf16),
            pltpu.VMEM((width, pts), bf16),
            pltpu.VMEM((width, pts), f32),
            pltpu.VMEM((QW, QW), bf16),
            pltpu.VMEM((QN, QW, QW), bf16),
            pltpu.VMEM((QN, QW, QW), bf16),
            pltpu.VMEM((2, H, W2 + 8, 2 * W), f32),
            pltpu.VMEM((2, 2, N, W2 + 8, 2 * W), f32),
            pltpu.VMEM((2, 2, N, W2 + 8, 2 * W), f32),
            pltpu.VMEM((2, H, W2 + 8, 2 * W), f32),
            pltpu.VMEM((2, W, 2 * W), f32),
            pltpu.VMEM((H, 8, pts), f32),
            pltpu.VMEM((ND, R, 4 * W), f32),
            pltpu.VMEM((ND, R, 2 * W), f32),
            pltpu.VMEM((3, max(N, ND), R, 4 * W), f32),
            pltpu.VMEM((3, max(N, ND), R, 2 * W), f32),
            dma((3, QN)),
            dma((3,)),
            dma((2,)),
            dma((2, 2)),
            dma((2,)),
            dma((2, 2)),
            dma((2,)),
            dma((2, 2)),
            dma((3,)),
            dma((3,)),
            dma((3,)),
            dma((3,)),
        ],
        compiler_params=pltpu.CompilerParams(
            collective_id=0, has_side_effects=True, vmem_limit_bytes=VMEM_LIMIT
        ),
    )(node, pool, cot, w, sharp, maps)
    each = H // ND
    return pl.pallas_call(
        functools.partial(finish_kernel, each),
        out_shape=(
            big,
            big,
            big,
            jax.ShapeDtypeStruct((R, W), f32),
            jax.ShapeDtypeStruct((each,), f32),
            jax.ShapeDtypeStruct((R, 3 * W), f32),
        ),
        in_specs=[vmem] * 4,
        out_specs=[any_] * 6,
        scratch_shapes=[
            pltpu.VMEM((R, W), f32),
            pltpu.VMEM((R, 3 * W), f32),
            pltpu.SMEM((each,), f32),
            dma((6,)),
        ],
        compiler_params=pltpu.CompilerParams(vmem_limit_bytes=VMEM_LIMIT),
    )(lo, gm, pc, small)


def solution(mesh):
    N = int(round(mesh.shape["point"] ** 0.5))
    ND = mesh.shape["dp"]
    big = P("dp", "point", None)
    return jax.shard_map(
        functools.partial(per_device, N, ND),
        mesh=mesh,
        in_specs=(big, big, big, P(), P(), P()),
        out_specs=(big, big, big, P("dp", None), P("dp"), P("dp", None)),
        check_vma=False,
    )
```

time: 76.3 us -> 59.4 us (0.78)
  the two profiles are of different devices: /device:TPU:6 before, /device:TPU:1 now
where the time goes in v2:
time: 59.4 us; the launch traced here: 59.3 us
  Pallas kernels  58.6 us (99%)
  between operations  0.64 us (1%)
    pallas_call x1, Pallas kernels, per_device(): pl.pallas_call(functools.partial(kernel, N, ND, H), out_shape=(big, big,...  57.2 us
    pallas_call x1, Pallas kernels, per_device(): pl.pallas_call(functools.partial(finish_kernel, each), out_shape=(big, bi...  1.47 us

profile of v2, /device:TPU:1, one launch (start us, length us, event | category | flops | bytes accessed | tf_op | source)
XLA Modules:
  0.0 59.3 jit_solution(10132883955091568419)
XLA Ops:
  0.6 57.2 %shard_map.109 = (bf16[1,384,1024]{2,1,0:T(8,128)(2,1)S(1)}, bf16[1,384,1024]{2,1,0:T(8,128)(2,1)S(1)}, bf16[1,384,1024]{2,1,0:T(8,128)(2,1)S(1)}, f32[8,384]{1,0:T(8,128)S(1)}) custom-call(bf16[1,384,1024]{2,1,0:T(8,128)(2,1)} %node_h.1, bf16[1,384,1024]{2,1,0:T(8,128)(2,1)} %pool_h.1, bf16[1,384,1024]{2,1,0:T(8,128)(2,1)} %cot_h.1, bf16[64,64]{1,0:T(8,128)(2,1)} %w_h.1, ...), custom_call_target="tpu_custom_call" | custom-call | tf_op jit(solution)/shard_map/pallas_call | solution.py:531
  57.8 1.5 %shard_map.110 = (bf16[1,384,1024]{2,1,0:T(8,128)(2,1)}, bf16[1,384,1024]{2,1,0:T(8,128)(2,1)}, bf16[1,384,1024]{2,1,0:T(8,128)(2,1)}, f32[8,64]{1,0:T(8,128)}, f32[2]{0:T(128)}, /*index=5*/f32[8,192]{1,0:T(8,128)}) custom-call(bf16[1,384,1024]{2,1,0:T(8,128)(2,1)S(1)} %get-tuple-element.10.lo_i, bf16[1,384,1024]{2,1,0:T(8,128)(2,1)S(1)} %get-tuple-element.11.gm_i, ...), custom_call_target="tpu_custom_call" | custom-call | tf_op jit(solution)/shard_map/pallas_call | solution.py:580

commit v3 on v2

--- a/solution.py
+++ b/solution.py
@@ -13,6 +13,7 @@
 W = 64
 Q = 4
 QW = Q * W
+BANDS = 1
 VMEM_LIMIT = 40 * 1024 * 1024
 NN = (((1,), (0,)), ((), ()))
 NT = (((1,), (1,)), ((), ()))
@@ -104,6 +105,9 @@
             return i * N + j if f == 0 else j * N + i
         return jnp.where(f == 0, i * N + j, j * N + i)
 
+    def far_first(n):
+        return sorted(range(1, n), key=lambda k: -min(k, n - k))
+
     def rcopy(src, dst, ssem, rsem, **dev):
         return pltpu.make_async_remote_copy(
             src_ref=src,
@@ -201,7 +205,7 @@
             point=place(f, i, second(f)),
         )
 
-    def forward(t, carry):
+    def forward(t):
         q = order(t)
         for c in fetch(q):
             c.wait()
@@ -230,8 +234,7 @@
             send1[0, q * Q + i, W2:, :] = m
             send1[1, q * Q + i, :W2, :] = fold(gmixed[r, c], i)
 
-        @pl.when(t == 0)
-        def _():
+        if t == 0:
             pl.semaphore_wait(barrier, 2 * (N - 1) + ND - 1)
 
         for s in range(2):
@@ -242,9 +245,8 @@
                 def _():
                     phase1(s, h, h // N, h % N).start()
 
-        return carry
-
-    lax.fori_loop(0, QN, forward, 0)
+    for t in range(QN):
+        forward(t)
 
     def flip(q):
         slb[:, lanes_of(q)] = slt[rows_of(q), :].T
@@ -268,7 +270,7 @@
         for i in range(1, N):
             part = part + recv1[s, f, i, :n, :]
         recv2[s, f, second(f), :n, :] = part
-        for k in range(1, N):
+        for k in far_first(N):
             phase2(s, f, (second(f) + k) % N).start()
 
     def arrived2(s, f):
@@ -298,7 +300,7 @@
         )
 
     def send3(s, f):
-        for k in range(1, N):
+        for k in far_first(N):
             phase3(s, f, (first(f) + k) % N).start()
 
     totals = [arrived2(0, f) for f in range(2)]
@@ -359,7 +361,7 @@
 
         def send(stage, source):
             me, n = axes[stage]
-            for k in range(1, n):
+            for k in far_first(n):
                 k = (me + k) % n
                 copy(stage, k, source(k)).start()
 
@@ -404,24 +406,26 @@
         for f in range(2):
             wait_bytes(res.at[s, pl.ds(0, N - 1), pl.ds(0, rows_out[s])], r3.at[s, f])
             if QN > 1:
-                lax.fori_loop(f * (QN // 2), (f + 1) * (QN // 2), body, 0)
+                for q in range(f * (QN // 2), (f + 1) * (QN // 2)):
+                    body(q)
         if QN == 1:
-            body(0, 0)
+            body(0)
 
     def pair(i):
         return slice(i // 2 * 2 * W, (i // 2 + 1) * 2 * W)
 
-    def with_mixed(q, carry):
+    def with_mixed(q):
         for i in range(Q):
             mbs[q, i * W : (i + 1) * W, pair(i)] = spread(res[0, q * Q + i, :W2, :], i).astype(bf16)
         gpart[rows_of(q), :] = bdot(mbs[q], cot[:, lanes_of(q)], NT)
         lo_ref[0, :, lanes_of(q)] = bdot(slb[:, lanes_of(q)], mbs[q]).astype(bf16)
-        return carry
 
     halves(0, with_mixed)
     t_onward(1)
 
-    def backward(q, carry):
+    quarter = lax.broadcasted_iota(jnp.int32, (8, 2 * W), 1) // W2
+
+    def backward(q):
         cols = []
         for i in range(Q):
             gbs[q, i * W : (i + 1) * W, pair(i)] = spread(res[1, q * Q + i, :W2, :], i).astype(bf16)
@@ -431,6 +435,7 @@
                         res[1, q * Q + i, W2 : W2 + 1, :] + res[1, q * Q + i + 1, W2 : W2 + 1, :]
                     )
                 )
+        part = None
         gq = gpart[rows_of(q), :] + bdot(gbs[q], pool[:, lanes_of(q)], NT)
         for i in range(Q):
             h = q * Q + i
@@ -440,27 +445,24 @@
             gz = sg - s * jnp.sum(sg, axis=0, keepdims=True)
             glt[rows_of(q, i, W), :] = (gz * inv_sharp(h, PTS)).astype(bf16)
             tz = gz * zed[rows_of(q, i, W), :]
-            tpart[h] = jnp.sum(tz.reshape(W // 8, 8, PTS), axis=0)
+            tz = jnp.sum(tz.reshape(W // 8, 8, PTS), axis=0)
+            tz = sum(tz[:, c : c + 2 * W] for c in range(0, PTS, 2 * W))
+            tz = tz + swap_halves(tz)
+            tz = (tz + pltpu.roll(tz, W2, 1)) * inv_sharp(h, 2 * W)
+            part = jnp.where(quarter == 2 + i % 2, -tz, part if i % 2 else 0.0)
+            if i % 2:
+                tpart[h // 2] = part
         gs = bdot(glt[rows_of(q), :], node[:, lanes_of(q)])
         for i in range(Q):
             acc[i % 2] += gs[i * W : (i + 1) * W, pair(i)]
-        return carry
 
     halves(1, backward)
 
     gst = jnp.where(low, acc[0] + swap_halves(acc[1]), 0.0)
     gst = jnp.concatenate([gst, jnp.zeros((W, 2 * W), f32)], axis=0).T[:W]
-    temps = []
-    for h in range(H):
-        v = jnp.sum(jnp.sum(tpart[h], axis=0, keepdims=True), axis=1, keepdims=True)
-        temps.append(-v * inv_sharp(h, 1))
-    each = H // ND
-    wide = lax.broadcasted_iota(jnp.int32, (R, 2 * W), 1)
     for d in range(ND):
-        v = gst[d * R : (d + 1) * R]
-        for n in range(each):
-            v = v + jnp.where(wide == W + n, temps[d * each + n], 0.0)
-        fin[d] = v
+        fin[d] = gst[d * R : (d + 1) * R]
+        fin[d, :8, :] = fin[d, :8, :] + tpart[d]
     f_begin(fin)
 
     def outputs(q):
@@ -484,7 +486,6 @@
 
 
 def finish_kernel(
-    each,
     lo_i,
     gm_i,
     pc_i,
@@ -500,16 +501,20 @@
     gt,
     sem,
 ):
-    pairs = [(lo_i, lo_h), (gm_i, gm_h), (pc_i, pc_h), (gs, gs_h), (gk, gk_h), (gt, gt_h)]
+    rows = lo_i.shape[1] // BANDS
+    pairs = [(gs, gs_h), (gk, gk_h), (gt, gt_h)]
+    for p in range(BANDS):
+        band = (0, pl.ds(p * rows, rows))
+        pairs += [(s.at[band], d.at[band]) for s, d in ((lo_i, lo_h), (gm_i, gm_h), (pc_i, pc_h))]
     copies = [pltpu.make_async_copy(s, d, sem.at[n]) for n, (s, d) in enumerate(pairs)]
-    for c in copies[:3]:
+    for c in copies[3:]:
         c.start()
     gs[...] = small[:, :W]
     gk[...] = small[:, 2 * W : 5 * W]
-    spot = lax.broadcasted_iota(jnp.int32, (1, 2 * W), 1)
-    for n in range(each):
-        gt[n] = jnp.sum(jnp.where(spot == W + n, small[:1, : 2 * W], 0.0))
-    for c in copies[3:]:
+    quarter = lax.broadcasted_iota(jnp.int32, (8, 2 * W), 1) // (W // 2)
+    for n in range(2):
+        gt[n] = jnp.sum(jnp.where(quarter == 2 + n, small[:8, : 2 * W], 0.0))
+    for c in copies[:3]:
         c.start()
     for c in copies:
         c.wait()
@@ -554,7 +559,7 @@
             pltpu.VMEM((2, 2, N, W2 + 8, 2 * W), f32),
             pltpu.VMEM((2, H, W2 + 8, 2 * W), f32),
             pltpu.VMEM((2, W, 2 * W), f32),
-            pltpu.VMEM((H, 8, pts), f32),
+            pltpu.VMEM((H // 2, 8, 2 * W), f32),
             pltpu.VMEM((ND, R, 4 * W), f32),
             pltpu.VMEM((ND, R, 2 * W), f32),
             pltpu.VMEM((3, max(N, ND), R, 4 * W), f32),
@@ -578,7 +583,7 @@
     )(node, pool, cot, w, sharp, maps)
     each = H // ND
     return pl.pallas_call(
-        functools.partial(finish_kernel, each),
+        finish_kernel,
         out_shape=(
             big,
             big,
@@ -593,7 +598,7 @@
             pltpu.VMEM((R, W), f32),
             pltpu.VMEM((R, 3 * W), f32),
             pltpu.SMEM((each,), f32),
-            dma((6,)),
+            dma((3 + 3 * BANDS,)),
         ],
         compiler_params=pltpu.CompilerParams(vmem_limit_bytes=VMEM_LIMIT),
     )(lo, gm, pc, small)

time: 59.4 us -> 56.6 us (0.953)
  Pallas kernels: 58.6 us -> 55.8 us
    pallas_call x1, Pallas kernels: 57.2 us -> 54.4 us  [per_device(): pl.pallas_call(functools.partial(kernel, N, ND, H), out_shape=(big, big,...]
where the time goes in v3:
time: 56.6 us; the launch traced here: 56.5 us
  Pallas kernels  55.8 us (99%)
  between operations  0.64 us (1%)
    pallas_call x1, Pallas kernels, per_device(): pl.pallas_call(functools.partial(kernel, N, ND, H), out_shape=(big, big,...  54.4 us
    pallas_call x1, Pallas kernels, per_device(): pl.pallas_call(finish_kernel, out_shape=(big, big, big, jax.ShapeDtypeStr...  1.45 us

profile of v3, /device:TPU:1, one launch (start us, length us, event | category | flops | bytes accessed | tf_op | source)
XLA Modules:
  0.0 56.5 jit_solution(601909917817612634)
XLA Ops:
  0.6 54.4 %shard_map.109 = (bf16[1,384,1024]{2,1,0:T(8,128)(2,1)S(1)}, bf16[1,384,1024]{2,1,0:T(8,128)(2,1)S(1)}, bf16[1,384,1024]{2,1,0:T(8,128)(2,1)S(1)}, f32[8,384]{1,0:T(8,128)S(1)}) custom-call(bf16[1,384,1024]{2,1,0:T(8,128)(2,1)} %node_h.1, bf16[1,384,1024]{2,1,0:T(8,128)(2,1)} %pool_h.1, bf16[1,384,1024]{2,1,0:T(8,128)(2,1)} %cot_h.1, bf16[64,64]{1,0:T(8,128)(2,1)} %w_h.1, ...), custom_call_target="tpu_custom_call" | custom-call | tf_op jit(solution)/shard_map/pallas_call | solution.py:536
  55.0 1.5 %shard_map.110 = (bf16[1,384,1024]{2,1,0:T(8,128)(2,1)}, bf16[1,384,1024]{2,1,0:T(8,128)(2,1)}, bf16[1,384,1024]{2,1,0:T(8,128)(2,1)}, f32[8,64]{1,0:T(8,128)}, f32[2]{0:T(128)}, /*index=5*/f32[8,192]{1,0:T(8,128)}) custom-call(bf16[1,384,1024]{2,1,0:T(8,128)(2,1)S(1)} %get-tuple-element.10.lo_i, bf16[1,384,1024]{2,1,0:T(8,128)(2,1)S(1)} %get-tuple-element.11.gm_i, ...), custom_call_target="tpu_custom_call" | custom-call | tf_op jit(solution)/shard_map/pallas_call | solution.py:585

commit v4 on v3

--- a/solution.py
+++ b/solution.py
@@ -121,6 +121,19 @@
     def wait_bytes(like, sem):
         pltpu.make_async_copy(like, like, sem).wait()
 
+    barrier = pltpu.get_barrier_semaphore()
+
+    def greet(**dev):
+        pl.semaphore_signal(
+            barrier, inc=1, device_id=dev, device_id_type=pl.DeviceIdType.MESH
+        )
+
+    for k in far_first(N):
+        greet(point=place(0, (me_y + k) % N, me_z))
+        greet(point=place(0, me_y, (me_z + k) % N))
+    for k in far_first(ND):
+        greet(dp=(me_d + k) % ND)
+
     def order(t):
         return (t % 2) * (QN // 2) + t // 2 if QN > 1 else t
 
@@ -140,20 +153,6 @@
     for t in range(QN):
         for c in fetch(order(t)):
             c.start()
-
-    barrier = pltpu.get_barrier_semaphore()
-    for k in range(1, N):
-        for dev in (place(0, (me_y + k) % N, me_z), place(0, me_y, (me_z + k) % N)):
-            pl.semaphore_signal(
-                barrier, inc=1, device_id={"point": dev}, device_id_type=pl.DeviceIdType.MESH
-            )
-    for k in range(1, ND):
-        pl.semaphore_signal(
-            barrier,
-            inc=1,
-            device_id={"dp": (me_d + k) % ND},
-            device_id_type=pl.DeviceIdType.MESH,
-        )
 
     for c in params:
         c.wait()
@@ -234,19 +233,16 @@
             send1[0, q * Q + i, W2:, :] = m
             send1[1, q * Q + i, :W2, :] = fold(gmixed[r, c], i)
 
-        if t == 0:
-            pl.semaphore_wait(barrier, 2 * (N - 1) + ND - 1)
-
-        for s in range(2):
-            for i in range(Q):
-                h = q * Q + i
-
-                @pl.when(h % N != first(h // N))
-                def _():
-                    phase1(s, h, h // N, h % N).start()
 
     for t in range(QN):
         forward(t)
+
+    pl.semaphore_wait(barrier, 2 * (N - 1) + ND - 1)
+    for s in range(2):
+        for k in far_first(N):
+            for f in range(2):
+                i = (first(f) + k) % N
+                phase1(s, f * N + i, f, i).start()
 
     def flip(q):
         slb[:, lanes_of(q)] = slt[rows_of(q), :].T

time: 56.6 us -> 53.3 us (0.942)
  Pallas kernels: 55.8 us -> 52.4 us
    pallas_call x1, Pallas kernels: 54.4 us -> 51 us  [per_device(): pl.pallas_call(functools.partial(kernel, N, ND, H), out_shape=(big, big,...]
where the time goes in v4:
time: 53.3 us; the launch traced here: 53.1 us
  Pallas kernels  52.4 us (98%)
  between operations  0.64 us (1%)
    pallas_call x1, Pallas kernels, per_device(): pl.pallas_call(functools.partial(kernel, N, ND, H), out_shape=(big, big,...  51 us
    pallas_call x1, Pallas kernels, per_device(): pl.pallas_call(finish_kernel, out_shape=(big, big, big, jax.ShapeDtypeStr...  1.45 us

profile of v4, /device:TPU:1, one launch (start us, length us, event | category | flops | bytes accessed | tf_op | source)
XLA Modules:
  0.0 53.1 jit_solution(11048930865919172019)
XLA Ops:
  0.6 51.0 %shard_map.109 = (bf16[1,384,1024]{2,1,0:T(8,128)(2,1)S(1)}, bf16[1,384,1024]{2,1,0:T(8,128)(2,1)S(1)}, bf16[1,384,1024]{2,1,0:T(8,128)(2,1)S(1)}, f32[8,384]{1,0:T(8,128)S(1)}) custom-call(bf16[1,384,1024]{2,1,0:T(8,128)(2,1)} %node_h.1, bf16[1,384,1024]{2,1,0:T(8,128)(2,1)} %pool_h.1, bf16[1,384,1024]{2,1,0:T(8,128)(2,1)} %cot_h.1, bf16[64,64]{1,0:T(8,128)(2,1)} %w_h.1, ...), custom_call_target="tpu_custom_call" | custom-call | tf_op jit(solution)/shard_map/pallas_call | solution.py:532
  51.6 1.5 %shard_map.110 = (bf16[1,384,1024]{2,1,0:T(8,128)(2,1)}, bf16[1,384,1024]{2,1,0:T(8,128)(2,1)}, bf16[1,384,1024]{2,1,0:T(8,128)(2,1)}, f32[8,64]{1,0:T(8,128)}, f32[2]{0:T(128)}, /*index=5*/f32[8,192]{1,0:T(8,128)}) custom-call(bf16[1,384,1024]{2,1,0:T(8,128)(2,1)S(1)} %get-tuple-element.10.lo_i, bf16[1,384,1024]{2,1,0:T(8,128)(2,1)S(1)} %get-tuple-element.11.gm_i, ...), custom_call_target="tpu_custom_call" | custom-call | tf_op jit(solution)/shard_map/pallas_call | solution.py:581

commit v5 on v4

--- a/solution.py
+++ b/solution.py
@@ -58,6 +58,7 @@
     slt,
     slb,
     glt,
+    nodet,
     gpart,
     bt,
     mbs,
@@ -66,7 +67,6 @@
     recv1,
     recv2,
     res,
-    acc,
     tpart,
     tgrad,
     fin,
@@ -128,33 +128,28 @@
             barrier, inc=1, device_id=dev, device_id_type=pl.DeviceIdType.MESH
         )
 
-    for k in far_first(N):
-        greet(point=place(0, (me_y + k) % N, me_z))
-        greet(point=place(0, me_y, (me_z + k) % N))
-    for k in far_first(ND):
-        greet(dp=(me_d + k) % ND)
-
-    def order(t):
-        return (t % 2) * (QN // 2) + t // 2 if QN > 1 else t
-
-    def fetch(q):
-        lanes = pl.ds(pl.multiple_of(q * QW, QW), QW)
-        return [
-            pltpu.make_async_copy(s.at[0, :, lanes], d.at[:, lanes], in_sem.at[n, q])
-            for n, (s, d) in enumerate(((node_h, node), (pool_h, pool), (cot_h, cot)))
-        ]
-
+    def greet_ring(steps):
+        for k in steps:
+            greet(point=place(0, (me_y + k) % N, me_z))
+            greet(point=place(0, me_y, (me_z + k) % N))
+
+    greet_ring(far_first(N)[:3])
+
+    inputs = [
+        pltpu.make_async_copy(s.at[0], d, in_sem.at[n])
+        for n, (s, d) in enumerate(((node_h, node), (pool_h, pool), (cot_h, cot)))
+    ]
     params = [
         pltpu.make_async_copy(s, d, par_sem.at[n])
         for n, (s, d) in enumerate(((w_h, w_ref), (sharp_h, sharp_ref), (maps_h, maps_ref)))
     ]
-    for c in params:
+    for c in params[:2] + inputs:
         c.start()
-    for t in range(QN):
-        for c in fetch(order(t)):
-            c.start()
-
-    for c in params:
+    greet_ring(far_first(N)[3:])
+    for k in far_first(ND):
+        greet(dp=(me_d + k) % ND)
+    params[2].start()
+    for c in params[:2]:
         c.wait()
     w4 = jnp.concatenate([w_ref[...].astype(f32)] * Q, axis=0)
     w4 = jnp.concatenate([w4] * Q, axis=1)
@@ -204,11 +199,7 @@
             point=place(f, i, second(f)),
         )
 
-    def forward(t):
-        q = order(t)
-        for c in fetch(q):
-            c.wait()
-        z = bdot(bt[...], node[:, lanes_of(q)], NT)
+    def soften(q, z):
         sums = []
         for i in range(Q):
             zh = z[i * W : (i + 1) * W] * inv_sharp(q * Q + i, PTS)
@@ -219,6 +210,9 @@
             sl[rows_of(q, i, W), :] = s
             slt[rows_of(q, i, W), :] = sb
             sums.append(sum(s[:, c : c + 2 * W] for c in range(0, PTS, 2 * W)))
+        return sums
+
+    def gather(q, sums):
         sq = slt[rows_of(q), :]
         sums = jnp.concatenate(sums, axis=0)
         top = sums.astype(bf16)
@@ -234,8 +228,13 @@
             send1[1, q * Q + i, :W2, :] = fold(gmixed[r, c], i)
 
 
-    for t in range(QN):
-        forward(t)
+    inputs[0].wait()
+    zs = [bdot(bt[...], node[:, lanes_of(q)], NT) for q in range(QN)]
+    sums_of = [soften(q, zs[q]) for q in range(QN)]
+    for c in inputs[1:]:
+        c.wait()
+    for q in range(QN):
+        gather(q, sums_of[q])
 
     pl.semaphore_wait(barrier, 2 * (N - 1) + ND - 1)
     for s in range(2):
@@ -244,11 +243,11 @@
                 i = (first(f) + k) % N
                 phase1(s, f * N + i, f, i).start()
 
-    def flip(q):
+    for q in range(QN):
         slb[:, lanes_of(q)] = slt[rows_of(q), :].T
-
-    for q in range(QN):
-        flip(q)
+        nodet[rows_of(q), :] = node[:, lanes_of(q)].T
+        mbs[q] = jnp.zeros((QW, QW), bf16)
+        gbs[q] = jnp.zeros((QW, QW), bf16)
 
     def phase2(s, f, j):
         mine = recv2.at[s, f, second(f), pl.ds(0, rows_in[s])]
@@ -281,11 +280,7 @@
         for f in range(2):
             arrived1(s, f)
 
-    for q in range(QN):
-        mbs[q] = jnp.zeros((QW, QW), bf16)
-        gbs[q] = jnp.zeros((QW, QW), bf16)
-    acc[...] = jnp.zeros(acc.shape, f32)
-
+    params[2].wait()
     maps = maps_ref[...]
 
     def phase3(s, f, i):
@@ -326,9 +321,9 @@
     gquery = hdot(gscore, key)
     gkey = hdot(gscore.T, query)
     gproj = jnp.concatenate([gquery, gkey, gvalue], axis=1)
-    gtok = hdot(gproj, maps, NT)
+    gtok = hdot(gvalue, maps[:, 2 * W :], NT) + hdot(gproj[:, : 2 * W], maps[:, : 2 * W], NT)
     gpool = (gtok * inverse).astype(bf16).astype(f32)
-    gmass = hdot(jnp.ones((8, W), f32), -(gtok * t) * inverse, NT)
+    gmass = hdot(jnp.ones((8, 3 * W), f32), -(gproj * proj) * inverse, NT)
     for f in range(2):
         h = f * N + first(f)
         res[1, h, :W2, :] = jnp.concatenate(
@@ -399,63 +394,72 @@
     t_begin(tgrad)
 
     def halves(s, body):
+        got = []
         for f in range(2):
             wait_bytes(res.at[s, pl.ds(0, N - 1), pl.ds(0, rows_out[s])], r3.at[s, f])
             if QN > 1:
-                for q in range(f * (QN // 2), (f + 1) * (QN // 2)):
-                    body(q)
+                got.append(body(range(f * (QN // 2), (f + 1) * (QN // 2))))
         if QN == 1:
-            body(0)
+            got.append(body(range(1)))
+        return got
 
     def pair(i):
         return slice(i // 2 * 2 * W, (i // 2 + 1) * 2 * W)
 
-    def with_mixed(q):
-        for i in range(Q):
-            mbs[q, i * W : (i + 1) * W, pair(i)] = spread(res[0, q * Q + i, :W2, :], i).astype(bf16)
-        gpart[rows_of(q), :] = bdot(mbs[q], cot[:, lanes_of(q)], NT)
-        lo_ref[0, :, lanes_of(q)] = bdot(slb[:, lanes_of(q)], mbs[q]).astype(bf16)
+    def with_mixed(groups):
+        for q in groups:
+            for i in range(Q):
+                block = spread(res[0, q * Q + i, :W2, :], i)
+                mbs[q, i * W : (i + 1) * W, pair(i)] = block.astype(bf16)
+        for q in groups:
+            gpart[rows_of(q), :] = bdot(mbs[q], cot[:, lanes_of(q)], NT)
+        for q in groups:
+            lo_ref[0, :, lanes_of(q)] = bdot(slb[:, lanes_of(q)], mbs[q]).astype(bf16)
 
     halves(0, with_mixed)
-    t_onward(1)
 
     quarter = lax.broadcasted_iota(jnp.int32, (8, 2 * W), 1) // W2
 
-    def backward(q):
-        cols = []
-        for i in range(Q):
-            gbs[q, i * W : (i + 1) * W, pair(i)] = spread(res[1, q * Q + i, :W2, :], i).astype(bf16)
-            if i % 2 == 0:
-                cols.append(
-                    column(
+    def backward(groups):
+        gqs, cols = {}, {}
+        for q in groups:
+            cols[q] = []
+            for i in range(Q):
+                block = spread(res[1, q * Q + i, :W2, :], i)
+                gbs[q, i * W : (i + 1) * W, pair(i)] = block.astype(bf16)
+                if i % 2 == 0:
+                    row = (
                         res[1, q * Q + i, W2 : W2 + 1, :] + res[1, q * Q + i + 1, W2 : W2 + 1, :]
                     )
-                )
-        part = None
-        gq = gpart[rows_of(q), :] + bdot(gbs[q], pool[:, lanes_of(q)], NT)
-        for i in range(Q):
-            h = q * Q + i
-            s = sl[rows_of(q, i, W), :]
-            g = gq[i * W : (i + 1) * W] + cols[i // 2][i % 2 * W : (i % 2 + 1) * W]
-            sg = s * g
-            gz = sg - s * jnp.sum(sg, axis=0, keepdims=True)
-            glt[rows_of(q, i, W), :] = (gz * inv_sharp(h, PTS)).astype(bf16)
-            tz = gz * zed[rows_of(q, i, W), :]
-            tz = jnp.sum(tz.reshape(W // 8, 8, PTS), axis=0)
-            tz = sum(tz[:, c : c + 2 * W] for c in range(0, PTS, 2 * W))
-            tz = tz + swap_halves(tz)
-            tz = (tz + pltpu.roll(tz, W2, 1)) * inv_sharp(h, 2 * W)
-            part = jnp.where(quarter == 2 + i % 2, -tz, part if i % 2 else 0.0)
-            if i % 2:
-                tpart[h // 2] = part
-        gs = bdot(glt[rows_of(q), :], node[:, lanes_of(q)])
-        for i in range(Q):
-            acc[i % 2] += gs[i * W : (i + 1) * W, pair(i)]
-
-    halves(1, backward)
-
-    gst = jnp.where(low, acc[0] + swap_halves(acc[1]), 0.0)
-    gst = jnp.concatenate([gst, jnp.zeros((W, 2 * W), f32)], axis=0).T[:W]
+                    cols[q].append(column(row))
+        for q in groups:
+            gqs[q] = gpart[rows_of(q), :] + bdot(gbs[q], pool[:, lanes_of(q)], NT)
+        for q in groups:
+            for i in range(Q):
+                h = q * Q + i
+                s = sl[rows_of(q, i, W), :]
+                g = gqs[q][i * W : (i + 1) * W] + cols[q][i // 2][i % 2 * W : (i % 2 + 1) * W]
+                sg = s * g
+                gz = sg - s * jnp.sum(sg, axis=0, keepdims=True)
+                glt[rows_of(q, i, W), :] = (gz * inv_sharp(h, PTS)).astype(bf16)
+                tz = gz * zed[rows_of(q, i, W), :]
+                tz = jnp.sum(tz.reshape(W // 8, 8, PTS), axis=0)
+                tz = sum(tz[:, c : c + 2 * W] for c in range(0, PTS, 2 * W))
+                tz = tz + swap_halves(tz)
+                tz = (tz + pltpu.roll(tz, W2, 1)) * inv_sharp(h, 2 * W)
+                part = jnp.where(quarter == 2 + i % 2, -tz, part if i % 2 else 0.0)
+                if i % 2:
+                    tpart[h // 2] = part
+        sides = [0.0, 0.0]
+        for q in groups:
+            gs = bdot(nodet[rows_of(q), :], glt[rows_of(q), :], NT)
+            for i in range(Q):
+                sides[i % 2] = sides[i % 2] + gs[i * W : (i + 1) * W, pair(i)]
+        return sides
+
+    left, right = (sum(x) for x in zip(*halves(1, backward)))
+
+    gst = jnp.where(low, left + swap_halves(right), 0.0)
     for d in range(ND):
         fin[d] = gst[d * R : (d + 1) * R]
         fin[d, :8, :] = fin[d, :8, :] + tpart[d]
@@ -466,10 +470,11 @@
         gm_ref[0, :, lanes_of(q)] = bdot(gl, bt[...]).astype(bf16)
         pc_ref[0, :, lanes_of(q)] = bdot(slb[:, lanes_of(q)], gbs[q]).astype(bf16)
 
-    t_onward(2)
+    t_onward(1)
     for q in range(QN):
         outputs(q)
     f_onward(1)
+    t_onward(2)
     for s in range(2):
         wait_bytes(send1.at[s, pl.ds(0, 2 * N - 2), pl.ds(0, rows_in[s])], s1.at[s])
         wait_bytes(recv2.at[s, :, pl.ds(0, N - 1), pl.ds(0, rows_in[s])], s2.at[s])
@@ -546,6 +551,7 @@
             pltpu.VMEM((width, pts), bf16),
             pltpu.VMEM((pts, width), bf16),
             pltpu.VMEM((width, pts), bf16),
+            pltpu.VMEM((width, pts), bf16),
             pltpu.VMEM((width, pts), f32),
             pltpu.VMEM((QW, QW), bf16),
             pltpu.VMEM((QN, QW, QW), bf16),
@@ -554,13 +560,12 @@
             pltpu.VMEM((2, 2, N, W2 + 8, 2 * W), f32),
             pltpu.VMEM((2, 2, N, W2 + 8, 2 * W), f32),
             pltpu.VMEM((2, H, W2 + 8, 2 * W), f32),
-            pltpu.VMEM((2, W, 2 * W), f32),
             pltpu.VMEM((H // 2, 8, 2 * W), f32),
             pltpu.VMEM((ND, R, 4 * W), f32),
             pltpu.VMEM((ND, R, 2 * W), f32),
             pltpu.VMEM((3, max(N, ND), R, 4 * W), f32),
             pltpu.VMEM((3, max(N, ND), R, 2 * W), f32),
-            dma((3, QN)),
+            dma((3,)),
             dma((3,)),
             dma((2,)),
             dma((2, 2)),

time: 53.3 us -> 52 us (0.976)
  Pallas kernels: 52.4 us -> 51 us
    pallas_call x1, Pallas kernels: 51 us -> 49.5 us  [per_device(): pl.pallas_call(functools.partial(kernel, N, ND, H), out_shape=(big, big,...]
where the time goes in v5:
time: 52 us; the launch traced here: 51.6 us
  Pallas kernels  51 us (98%)
  between operations  0.64 us (1%)
    pallas_call x1, Pallas kernels, per_device(): pl.pallas_call(functools.partial(kernel, N, ND, H), out_shape=(big, big,...  49.5 us
    pallas_call x1, Pallas kernels, per_device(): pl.pallas_call(finish_kernel, out_shape=(big, big, big, jax.ShapeDtypeStr...  1.45 us

profile of v5, /device:TPU:1, one launch (start us, length us, event | category | flops | bytes accessed | tf_op | source)
XLA Modules:
  0.0 51.6 jit_solution(12789021860291834858)
XLA Ops:
  0.6 49.5 %shard_map.109 = (bf16[1,384,1024]{2,1,0:T(8,128)(2,1)S(1)}, bf16[1,384,1024]{2,1,0:T(8,128)(2,1)S(1)}, bf16[1,384,1024]{2,1,0:T(8,128)(2,1)S(1)}, f32[8,384]{1,0:T(8,128)S(1)}) custom-call(bf16[1,384,1024]{2,1,0:T(8,128)(2,1)} %node_h.1, bf16[1,384,1024]{2,1,0:T(8,128)(2,1)} %pool_h.1, bf16[1,384,1024]{2,1,0:T(8,128)(2,1)} %cot_h.1, bf16[64,64]{1,0:T(8,128)(2,1)} %w_h.1, ...), custom_call_target="tpu_custom_call" | custom-call | tf_op jit(solution)/shard_map/pallas_call | solution.py:537
  50.2 1.5 %shard_map.110 = (bf16[1,384,1024]{2,1,0:T(8,128)(2,1)}, bf16[1,384,1024]{2,1,0:T(8,128)(2,1)}, bf16[1,384,1024]{2,1,0:T(8,128)(2,1)}, f32[8,64]{1,0:T(8,128)}, f32[2]{0:T(128)}, /*index=5*/f32[8,192]{1,0:T(8,128)}) custom-call(bf16[1,384,1024]{2,1,0:T(8,128)(2,1)S(1)} %get-tuple-element.10.lo_i, bf16[1,384,1024]{2,1,0:T(8,128)(2,1)S(1)} %get-tuple-element.11.gm_i, ...), custom_call_target="tpu_custom_call" | custom-call | tf_op jit(solution)/shard_map/pallas_call | solution.py:586

commit v6 on v5

--- a/solution.py
+++ b/solution.py
@@ -195,7 +195,7 @@
             send1.at[s, h, n],
             recv1.at[s, f, first(f), n],
             s1.at[s],
-            r1.at[s, f],
+            r1.at[s],
             point=place(f, i, second(f)),
         )
 
@@ -252,33 +252,36 @@
     def phase2(s, f, j):
         mine = recv2.at[s, f, second(f), pl.ds(0, rows_in[s])]
         return rcopy(
-            mine, mine, s2.at[s], r2.at[s, f], point=place(f, first(f), j)
-        )
-
-    def arrived1(s, f):
-        h = f * N + first(f)
-        own = send1[s, h]
-        recv1[s, f, first(f)] = own
-        wait_bytes(recv1.at[s, f, pl.ds(0, N - 1), pl.ds(0, rows_in[s])], r1.at[s, f])
+            mine, mine, s2.at[s], r2.at[s], point=place(f, first(f), j)
+        )
+
+    def arrived1(s):
         n = rows_in[s]
-        part = recv1[s, f, 0, :n, :]
-        for i in range(1, N):
-            part = part + recv1[s, f, i, :n, :]
-        recv2[s, f, second(f), :n, :] = part
+        for f in range(2):
+            recv1[s, f, first(f)] = send1[s, f * N + first(f)]
+        wait_bytes(recv1.at[s, :, pl.ds(0, N - 1), pl.ds(0, n)], r1.at[s])
+        for f in range(2):
+            part = recv1[s, f, 0, :n, :]
+            for i in range(1, N):
+                part = part + recv1[s, f, i, :n, :]
+            recv2[s, f, second(f), :n, :] = part
         for k in far_first(N):
-            phase2(s, f, (second(f) + k) % N).start()
-
-    def arrived2(s, f):
+            for f in range(2):
+                phase2(s, f, (second(f) + k) % N).start()
+
+    def arrived2(s):
         n = rows_in[s]
-        wait_bytes(recv2.at[s, f, pl.ds(0, N - 1), pl.ds(0, n)], r2.at[s, f])
-        total = recv2[s, f, 0, :n, :]
-        for j in range(1, N):
-            total = total + recv2[s, f, j, :n, :]
-        return total
+        wait_bytes(recv2.at[s, :, pl.ds(0, N - 1), pl.ds(0, n)], r2.at[s])
+        totals = []
+        for f in range(2):
+            total = recv2[s, f, 0, :n, :]
+            for j in range(1, N):
+                total = total + recv2[s, f, j, :n, :]
+            totals.append(total)
+        return totals
 
     for s in range(2):
-        for f in range(2):
-            arrived1(s, f)
+        arrived1(s)
 
     params[2].wait()
     maps = maps_ref[...]
@@ -287,14 +290,15 @@
         h = f * N + first(f)
         mine = res.at[s, h, pl.ds(0, rows_out[s])]
         return rcopy(
-            mine, mine, s3.at[s], r3.at[s, f], point=place(f, i, second(f))
-        )
-
-    def send3(s, f):
+            mine, mine, s3.at[s], r3.at[s], point=place(f, i, second(f))
+        )
+
+    def send3(s):
         for k in far_first(N):
-            phase3(s, f, (first(f) + k) % N).start()
-
-    totals = [arrived2(0, f) for f in range(2)]
+            for f in range(2):
+                phase3(s, f, (first(f) + k) % N).start()
+
+    totals = arrived2(0)
     mass = jnp.concatenate([total[W2:] for total in totals], axis=0)
     mass = jnp.concatenate([mass, jnp.ones((6, 2 * W), f32)], axis=0).T
     inverse = 1.0 / (jnp.concatenate([mass[:W, :1], mass[:W, 1:2]], axis=0) + epsilon)
@@ -312,9 +316,9 @@
         res[0, f * N + first(f), :W2, :] = jnp.concatenate(
             [mixed[f * W : f * W + W2], mixed[f * W + W2 : (f + 1) * W]], axis=1
         )
-        send3(0, f)
-
-    gmix = jnp.concatenate([unfold(arrived2(1, f)) for f in range(2)], axis=0)
+    send3(0)
+
+    gmix = jnp.concatenate([unfold(total) for total in arrived2(1)], axis=0)
     gattn = hdot(gmix, value, NT)
     gvalue = hdot(attn.T, gmix)
     gscore = attn * (gattn - jnp.sum(attn * gattn, axis=1, keepdims=True)) * W**-0.5
@@ -334,7 +338,7 @@
         res[1, h, W2:, :] = jnp.where(
             even, jnp.where(low[:8], here, 0.0), jnp.where(low[:8], 0.0, there)
         )
-        send3(1, f)
+    send3(1)
 
     def all_of(buf, ssem, rsem):
         axes = ((me_d, ND), (me_z, N), (me_y, N))
@@ -347,7 +351,7 @@
         def copy(stage, k, src):
             me = axes[stage][0]
             return rcopy(
-                src, buf.at[stage, me], ssem.at[stage], rsem.at[stage], **dev(stage, k)
+                src, buf.at[stage, me], ssem.at[0], rsem.at[stage], **dev(stage, k)
             )
 
         def send(stage, source):
@@ -378,9 +382,10 @@
             return receive(2)
 
         def drain():
-            for stage in range(3):
-                n = axes[stage][1]
-                wait_bytes(buf.at[stage, pl.ds(0, n - 1)], ssem.at[stage])
+            if N == ND:
+                wait_bytes(buf.at[:, pl.ds(0, N - 1)], ssem.at[0])
+            else:
+                raise NotImplementedError
 
         return begin, onward, finish, drain
 
@@ -393,15 +398,8 @@
         tgrad[d] = tg[d * R : (d + 1) * R]
     t_begin(tgrad)
 
-    def halves(s, body):
-        got = []
-        for f in range(2):
-            wait_bytes(res.at[s, pl.ds(0, N - 1), pl.ds(0, rows_out[s])], r3.at[s, f])
-            if QN > 1:
-                got.append(body(range(f * (QN // 2), (f + 1) * (QN // 2))))
-        if QN == 1:
-            got.append(body(range(1)))
-        return got
+    def await3(s):
+        wait_bytes(res.at[s, pl.ds(0, 2 * N - 2), pl.ds(0, rows_out[s])], r3.at[s])
 
     def pair(i):
         return slice(i // 2 * 2 * W, (i // 2 + 1) * 2 * W)
@@ -416,7 +414,8 @@
         for q in groups:
             lo_ref[0, :, lanes_of(q)] = bdot(slb[:, lanes_of(q)], mbs[q]).astype(bf16)
 
-    halves(0, with_mixed)
+    await3(0)
+    with_mixed(range(QN))
 
     quarter = lax.broadcasted_iota(jnp.int32, (8, 2 * W), 1) // W2
 
@@ -457,7 +456,8 @@
                 sides[i % 2] = sides[i % 2] + gs[i * W : (i + 1) * W, pair(i)]
         return sides
 
-    left, right = (sum(x) for x in zip(*halves(1, backward)))
+    await3(1)
+    left, right = backward(range(QN))
 
     gst = jnp.where(low, left + swap_halves(right), 0.0)
     for d in range(ND):
@@ -568,14 +568,14 @@
             dma((3,)),
             dma((3,)),
             dma((2,)),
-            dma((2, 2)),
             dma((2,)),
-            dma((2, 2)),
             dma((2,)),
-            dma((2, 2)),
+            dma((2,)),
+            dma((2,)),
+            dma((2,)),
+            dma((1,)),
             dma((3,)),
-            dma((3,)),
-            dma((3,)),
+            dma((1,)),
             dma((3,)),
         ],
         compiler_params=pltpu.CompilerParams(

time: 52 us -> 51.6 us (level)
  no operation moved by 1% of the time
where the time goes in v6:
time: 51.6 us; the launch traced here: 51.5 us
  Pallas kernels  50.8 us (98%)
  between operations  0.64 us (1%)
    pallas_call x1, Pallas kernels, per_device(): pl.pallas_call(functools.partial(kernel, N, ND, H), out_shape=(big, big,...  49.4 us
    pallas_call x1, Pallas kernels, per_device(): pl.pallas_call(finish_kernel, out_shape=(big, big, big, jax.ShapeDtypeStr...  1.45 us

profile of v6, /device:TPU:1, one launch (start us, length us, event | category | flops | bytes accessed | tf_op | source)
XLA Modules:
  0.0 51.5 jit_solution(6886155902312350776)
XLA Ops:
  0.6 49.4 %shard_map.109 = (bf16[1,384,1024]{2,1,0:T(8,128)(2,1)S(1)}, bf16[1,384,1024]{2,1,0:T(8,128)(2,1)S(1)}, bf16[1,384,1024]{2,1,0:T(8,128)(2,1)S(1)}, f32[8,384]{1,0:T(8,128)S(1)}) custom-call(bf16[1,384,1024]{2,1,0:T(8,128)(2,1)} %node_h.1, bf16[1,384,1024]{2,1,0:T(8,128)(2,1)} %pool_h.1, bf16[1,384,1024]{2,1,0:T(8,128)(2,1)} %cot_h.1, bf16[64,64]{1,0:T(8,128)(2,1)} %w_h.1, ...), custom_call_target="tpu_custom_call" | custom-call | tf_op jit(solution)/shard_map/pallas_call | solution.py:537
  50.0 1.5 %shard_map.110 = (bf16[1,384,1024]{2,1,0:T(8,128)(2,1)}, bf16[1,384,1024]{2,1,0:T(8,128)(2,1)}, bf16[1,384,1024]{2,1,0:T(8,128)(2,1)}, f32[8,64]{1,0:T(8,128)}, f32[2]{0:T(128)}, /*index=5*/f32[8,192]{1,0:T(8,128)}) custom-call(bf16[1,384,1024]{2,1,0:T(8,128)(2,1)S(1)} %get-tuple-element.10.lo_i, bf16[1,384,1024]{2,1,0:T(8,128)(2,1)S(1)} %get-tuple-element.11.gm_i, ...), custom_call_target="tpu_custom_call" | custom-call | tf_op jit(solution)/shard_map/pallas_call | solution.py:586

commit v7 on v6

--- a/solution.py
+++ b/solution.py
@@ -411,8 +411,6 @@
                 mbs[q, i * W : (i + 1) * W, pair(i)] = block.astype(bf16)
         for q in groups:
             gpart[rows_of(q), :] = bdot(mbs[q], cot[:, lanes_of(q)], NT)
-        for q in groups:
-            lo_ref[0, :, lanes_of(q)] = bdot(slb[:, lanes_of(q)], mbs[q]).astype(bf16)
 
     await3(0)
     with_mixed(range(QN))
@@ -467,6 +465,7 @@
 
     def outputs(q):
         gl = glt[rows_of(q), :].T
+        lo_ref[0, :, lanes_of(q)] = bdot(slb[:, lanes_of(q)], mbs[q]).astype(bf16)
         gm_ref[0, :, lanes_of(q)] = bdot(gl, bt[...]).astype(bf16)
         pc_ref[0, :, lanes_of(q)] = bdot(slb[:, lanes_of(q)], gbs[q]).astype(bf16)
 

time: 51.6 us -> 51.6 us (level)
  no operation moved by 1% of the time
where the time goes in v7:
time: 51.6 us; the launch traced here: 51.5 us
  Pallas kernels  50.8 us (98%)
  between operations  0.64 us (1%)
    pallas_call x1, Pallas kernels, per_device(): pl.pallas_call(functools.partial(kernel, N, ND, H), out_shape=(big, big,...  49.4 us
    pallas_call x1, Pallas kernels, per_device(): pl.pallas_call(finish_kernel, out_shape=(big, big, big, jax.ShapeDtypeStr...  1.45 us

profile of v7, /device:TPU:1, one launch (start us, length us, event | category | flops | bytes accessed | tf_op | source)
XLA Modules:
  0.0 51.5 jit_solution(12706192214594534701)
XLA Ops:
  0.6 49.4 %shard_map.109 = (bf16[1,384,1024]{2,1,0:T(8,128)(2,1)S(1)}, bf16[1,384,1024]{2,1,0:T(8,128)(2,1)S(1)}, bf16[1,384,1024]{2,1,0:T(8,128)(2,1)S(1)}, f32[8,384]{1,0:T(8,128)S(1)}) custom-call(bf16[1,384,1024]{2,1,0:T(8,128)(2,1)} %node_h.1, bf16[1,384,1024]{2,1,0:T(8,128)(2,1)} %pool_h.1, bf16[1,384,1024]{2,1,0:T(8,128)(2,1)} %cot_h.1, bf16[64,64]{1,0:T(8,128)(2,1)} %w_h.1, ...), custom_call_target="tpu_custom_call" | custom-call | tf_op jit(solution)/shard_map/pallas_call | solution.py:536
  50.0 1.5 %shard_map.110 = (bf16[1,384,1024]{2,1,0:T(8,128)(2,1)}, bf16[1,384,1024]{2,1,0:T(8,128)(2,1)}, bf16[1,384,1024]{2,1,0:T(8,128)(2,1)}, f32[8,64]{1,0:T(8,128)}, f32[2]{0:T(128)}, /*index=5*/f32[8,192]{1,0:T(8,128)}) custom-call(bf16[1,384,1024]{2,1,0:T(8,128)(2,1)S(1)} %get-tuple-element.10.lo_i, bf16[1,384,1024]{2,1,0:T(8,128)(2,1)S(1)} %get-tuple-element.11.gm_i, ...), custom_call_target="tpu_custom_call" | custom-call | tf_op jit(solution)/shard_map/pallas_call | solution.py:585
